TPU v7x, 128 devices: a whole 4x4x4 slice. The times are simulated.
128 devices in a mesh: wide: 32 (over x, y, core), narrow: 4 (over z).
Axes of the slice: x: 4, y: 4, z: 4, core: 2. Of those that a mesh axis runs over, the one named last changes fastest.
Arguments:
- features: bfloat16 [512, 32, 32, 8, 128], P('wide', None, 'narrow'), may hold values from -6 to 6
- occupied: int32 [512], P('wide'), may hold values from 0 to 1, as said below
- w_first: bfloat16 [32, 32, 3, 3, 3], replicated, may hold values from -0.21875 to 0.21875
- w_second: bfloat16 [32, 32, 3, 3, 3], replicated, may hold values from -0.21875 to 0.21875
- w_head: bfloat16 [3, 32], replicated, may hold values from -1 to 1
Outputs:
- affinities: bfloat16 [512, 3, 32, 8, 128], P('wide', None, 'narrow')
Inputs may be any that keep to these rules, and one draw needn't show every extreme that they name: Some index of wide has all 16 of its blocks occupied; in all, between (5) * 32 + 2 and 192 blocks are occupied.
All inputs are finite; a program needn't handle non-finite values.
Results may differ from a plain program's by a relative error of at most 0.0051.
Values may be sent and summed in bfloat16 or wider, within the bound.
A program may use at most 128 MiB of HBM per device.

v0:
```python
import jax
import jax.numpy as jnp
from jax import lax
from jax.sharding import PartitionSpec as P

MARGIN = 2
CAP = 6


def padded_2(cells, sides, width):
    for axis, dim in sides:
        count = lax.axis_size(axis)
        ends = count - 1
        head = lax.slice_in_dim(cells, 0, width, axis=dim)
        tail = lax.slice_in_dim(cells, cells.shape[dim] - width, cells.shape[dim], axis=dim)
        cells = jnp.concatenate(
            [
                lax.ppermute(tail, axis, [(i, (i + 1) % count) for i in range(ends)]),
                cells,
                lax.ppermute(head, axis, [((i + 1) % count, i) for i in range(ends)]),
            ],
            axis=dim,
        )
    return cells


def shortened(value):

    def short(part):
        return part.astype(jnp.bfloat16) if part.dtype == jnp.float32 else part

    return jax.tree.map(short, value)


def blend_table(tile_depth):
    places = jnp.arange(tile_depth).astype(jnp.float32)
    rising = (places + 0.5) / (2 * MARGIN)
    falling = (tile_depth - places - 0.5) / (2 * MARGIN)
    return jnp.minimum(1.0, jnp.minimum(rising, falling))


def cover_table(narrow_index, narrow_size, planes):
    blending = blend_table(planes + 2 * MARGIN)
    within = jnp.arange(planes)
    own_part = blending[within + MARGIN]
    lower_part = blending[jnp.minimum(within + planes + MARGIN, planes + 2 * MARGIN - 1)]
    upper_part = blending[jnp.maximum(within + MARGIN - planes, 0)]
    from_lower = jnp.where((within < MARGIN) & (narrow_index > 0), lower_part, 0.0)
    from_upper = jnp.where(
        (within >= planes - MARGIN) & (narrow_index < narrow_size - 1), upper_part, 0.0
    )
    return own_part + from_lower + from_upper


def convolve(inputs, kernel):
    return lax.conv_general_dilated(
        inputs,
        kernel,
        (1, 1, 1),
        "SAME",
        dimension_numbers=("NCDHW", "OIDHW", "NCDHW"),
        preferred_element_type=jnp.float32,
    )


def network(blocks_in, w_first, w_second, w_head):
    blending = blend_table(blocks_in.shape[2])

    def single_block(block):
        single = block[None]
        first_act = jax.nn.relu(convolve(single, w_first)).astype(jnp.bfloat16)
        second_act = jax.nn.relu(convolve(first_act, w_second) + single.astype(jnp.float32)).astype(
            jnp.bfloat16
        )
        logits = jnp.einsum(
            "ac,nczyx->nazyx", w_head, second_act, preferred_element_type=jnp.float32
        )
        return (logits * blending[None, None, :, None, None])[0]

    return lax.map(single_block, blocks_in)


def widen_blocks(blocks):
    return padded_2(blocks, (("narrow", 2),), MARGIN)


def fold_margins(weighted):
    padded = padded_2(shortened(weighted), (("narrow", 2),), MARGIN).astype(weighted.dtype)
    tile_depth = weighted.shape[2]
    interior = weighted[:, :, MARGIN : tile_depth - MARGIN]
    planes = tile_depth - 2 * MARGIN
    middle = jnp.zeros(
        interior.shape[:2] + (planes - 2 * MARGIN,) + interior.shape[3:], jnp.float32
    )
    additions = jnp.concatenate(
        [padded[:, :, :MARGIN], middle, padded[:, :, tile_depth + MARGIN :]], axis=2
    )
    return interior + additions


def on_device(features, occupied, w_first, w_second, w_head):
    home_slots = features.shape[0]
    planes = features.shape[2]
    breadth = lax.axis_size("wide")
    column = lax.axis_index("wide")
    narrow_size = lax.axis_size("narrow")
    narrow_index = lax.axis_index("narrow")
    per_peer = (home_slots + breadth - 1) // breadth
    lane_total = breadth * per_peer
    holding = jnp.sum(occupied).reshape(1)
    column_loads = lax.all_gather(holding, "wide", axis=0, tiled=True)
    offsets = jnp.cumsum(column_loads) - column_loads
    overall = jnp.sum(column_loads)
    my_offset = offsets[column]
    running = jnp.cumsum(occupied)
    local_rank = running - occupied
    lane_ids = jnp.arange(lane_total)
    peer_ids = lane_ids // per_peer
    peer_slot = lane_ids % per_peer
    wanted = (peer_ids - my_offset - overall) % breadth + peer_slot * breadth
    present = wanted < holding[0]
    picked = jnp.sum((running[None, :] <= wanted[:, None]).astype(jnp.int32), axis=1)
    source = widen_blocks(features)
    outgoing = jnp.take(source, jnp.minimum(picked, home_slots - 1), axis=0)
    outgoing = jnp.where(
        present[:, None, None, None, None], outgoing, jnp.zeros((), outgoing.dtype)
    )
    arrived = lax.all_to_all(
        outgoing.reshape((breadth, per_peer) + outgoing.shape[1:]),
        "wide",
        split_axis=0,
        concat_axis=0,
        tiled=True,
    )
    arrived = arrived.reshape(outgoing.shape)
    first_rank = (column - overall) % breadth
    work_ids = jnp.arange(CAP)
    work_ranks = first_rank + work_ids * breadth
    work_live = work_ranks < overall
    finishes = offsets + column_loads
    sender = jnp.sum((finishes[None, :] <= work_ranks[:, None]).astype(jnp.int32), axis=1)
    sender = jnp.minimum(sender, breadth - 1)
    lane_in = sender * per_peer + (work_ranks - offsets[sender]) // breadth
    blocks_in = jnp.take(arrived, jnp.clip(lane_in, 0, lane_total - 1), axis=0)
    blocks_in = jnp.where(
        work_live[:, None, None, None, None], blocks_in, jnp.zeros((), blocks_in.dtype)
    )
    weighted = network(blocks_in, w_first, w_second, w_head)
    sender_start = offsets[peer_ids]
    lane_rank = sender_start + (column - overall - sender_start) % breadth + peer_slot * breadth
    valid_back = lane_rank < sender_start + column_loads[peer_ids]
    slot_back = (lane_rank - first_rank) // breadth
    backward = jnp.take(weighted, jnp.clip(slot_back, 0, CAP - 1), axis=0)
    backward = jnp.where(valid_back[:, None, None, None, None], backward, 0.0)
    returned = lax.all_to_all(
        backward.reshape((breadth, per_peer) + backward.shape[1:]),
        "wide",
        split_axis=0,
        concat_axis=0,
        tiled=True,
    )
    returned = returned.reshape(backward.shape)
    destination = (my_offset + local_rank + overall) % breadth
    home_lane = destination * per_peer + local_rank // breadth
    home_result = jnp.take(returned, jnp.clip(home_lane, 0, lane_total - 1), axis=0)
    home_result = jnp.where((occupied > 0)[:, None, None, None, None], home_result, 0.0)
    home_result = fold_margins(home_result)
    coverage = cover_table(narrow_index, narrow_size, planes)
    return (home_result / coverage[None, None, :, None, None]).astype(jnp.bfloat16)


def solution(mesh):
    in_specs = (P("wide", None, "narrow", None, None), P("wide"), P(), P(), P())
    out_specs = P("wide", None, "narrow", None, None)
    return jax.shard_map(
        on_device, mesh=mesh, in_specs=in_specs, out_specs=out_specs, check_vma=False
    )
```

profile of v0, /device:TPU:0, one launch (start us, length us, event | category | flops | bytes accessed | tf_op | source)
XLA Modules:
  0.0 833.7 jit_solution(14977097107009091743)
XLA Ops:
  0.0 5.4 fusion.78
  5.4 4.0 collective-permute-start
  9.4 1.3 collective-permute-start.1
  12.0 1.3 dynamic-update-slice
  13.3 16.9 %all-reduce = s32[32]{0:T(128)S(1)} all-reduce(s32[32]{0:T(128)S(1)} %dynamic-update-slice), channel_id=1, replica_groups=mesh['wide'=32,'narrow'=4] {'wide'}, use_global_device_ids=true, to_apply=%add | all-reduce | flops 32 | bytes 256
  32.0 1.9 broadcast_compare_fusion
  34.0 20.5 %collective-permute-done = bf16[16,32,2,8,128]{4,3,2,1,0:T(8,128)(2,1)S(1)} collective-permute-done((bf16[16,32,2,8,128]{4,3,2,1,0:T(8,128)(2,1)}, bf16[16,32,2,8,128]{4,3,2,1,0:T(8,128)(2,1)S(1)}, u32[]{:S(2)}, u32[]{:S(2)}) %collective-permute-start) | collective-permute-done | bytes 2097184 | tf_op jit(solution)/shard_map/ppermute | solution.py:18
  54.5 4.3 collective-permute-done.1
  58.8 12.9 %pad_maximum_fusion = bf16[16,32,12,8,128]{4,3,2,1,0:T(8,128)(2,1)} fusion(bf16[16,32,2,8,128]{4,3,2,1,0:T(8,128)(2,1)} %collective-permute-done.1, bf16[16,32,8,8,128]{4,3,2,1,0:T(8,128)(2,1)} %param.7, bf16[16,32,2,8,128]{4,3,2,1,0:T(8,128)(2,1)S(1)} %collective-permute-done), kind=kLoop, calls=%fused_computation.60 | loop fusion | flops 12582912 | bytes 25165824 | tf_op jit(solution)/shard_map/concatenate | solution.py:16
  71.7 14.3 %gather_fusion.3 = bf16[32,32,12,8,128]{4,3,2,1,0:T(8,128)(2,1)} fusion(bf16[16,32,12,8,128]{4,3,2,1,0:T(8,128)(2,1)} %pad_maximum_fusion, s32[1024]{0:T(1024)S(1)} %pad_clamp_fusion.6), kind=kCustom, calls=%fused_computation.3 | custom fusion | bytes 50331776 | tf_op jit(solution)/shard_map/jit(_take)/gather | solution.py:124
  86.0 21.6 %fusion.52 = bf16[32,1,32,12,8,128]{5,4,3,2,1,0:T(8,128)(2,1)} fusion(bf16[32,32,12,8,128]{4,3,2,1,0:T(8,128)(2,1)} %gather_fusion.3, pred[32]{0:T(512)(128)(4,1)S(1)} %compare_and_fusion, pred[32]{0:T(512)(128)(4,1)S(1)} %get-tuple-element.99), kind=kLoop, calls=%fused_computation.59 | loop fusion | flops 25165824 | bytes 50331712 | tf_op jit(solution)/shard_map/jit(_where)/select_n | solution.py:125
  107.6 7.8 all-to-all-start
  120.8 357.5 %all-to-all-done = bf16[32,1,32,12,8,128]{5,4,3,2,1,0:T(8,128)(2,1)} async-done(((bf16[32,1,32,12,8,128]{5,4,3,2,1,0:T(8,128)(2,1)}), bf16[32,1,32,12,8,128]{5,4,3,2,1,0:T(8,128)(2,1)}, u32[]{:S(2)}, u32[]{:S(2)}) %all-to-all-start) | async-done | bytes 25165856 | tf_op jit(solution)/shard_map/all_to_all | solution.py:128
  478.3 11.6 %gather_fusion.4 = bf16[6,32,12,8,128]{4,3,2,1,0:T(8,128)(2,1)} fusion(bf16[32,32,12,8,128]{4,3,2,1,0:T(8,128)(2,1)} %bitcast.10, s32[1024]{0:T(1024)S(1)} %pad_clamp_fusion.5), kind=kCustom, calls=%fused_computation.4 | custom fusion | bytes 9437208 | tf_op jit(solution)/shard_map/jit(_take)/gather | solution.py:144
  489.9 5.1 select_select_fusion
  495.1 198.6 %while.11 = (s32[]{:T(128)}, f32[6,3,12,8,128]{4,3,2,1,0:T(8,128)}, bf16[6,32,12,8,128]{4,3,2,1,0:T(8,128)(2,1)}, bf16[32,32,3,3,3]{1,0,4,3,2:T(8,128)(2,1)S(1)}...) while((s32[]{:T(128)}, f32[6,3,12,8,128]{4,3,2,1,0:T(8,128)}, ...), condition=%wide.region_7.8_spmd.clone, body=%wide.region_6.7_spmd.clone.sunk | while | flops 1263145088 | bytes 19182632 | solution.py:80
  495.3 2.1 constant_dynamic-slice_fusion.2
  497.3 3.6 copy.61
  502.4 11.8 %fusion.100 = bf16[12,8,1,8,17,32]{5,3,4,1,0,2:T(8,128)(2,1)S(1)} fusion(pred[8,17]{0,1:T(8,128)(4,1)S(1)} %get-tuple-element.180, bf16[32,32,3,3,3]{1,0,4,3,2:T(8,128)(2,1)S(1)} %get-tuple-element.176, bf16[32,12,8,1,7,2]{0,4,5,2,1,3:T(8,128)(2,1)S(1)} %slice.90, bf16[32,12,8,1,8,17]{0,4,5,2,1,3:T(8,128)(2,1)S(1)} %copy.62), kind=kOutput, calls=%fused_computation.38.clone.1 | convolution fusion | flops 629489664 | bytes 1812616 | tf_op jit(solution)/shard_map/while/body/eval_jaxpr/conv_general_dilated | solution.py:56
  514.3 10.3 %fusion.102 = f32[12,8,8,17,32]{4,2,3,1,0:T(8,128)S(1)} fusion(bf16[32,32,3,3,3]{1,0,4,3,2:T(8,128)(2,1)S(1)} %copy-done.7, bf16[12,8,1,7,1,32]{5,3,4,1,0,2:T(8,128)(2,1)S(1)} %get-tuple-element.153, bf16[12,8,1,7,1,32]{5,3,4,1,0,2:T(8,128)(2,1)S(1)} %get-tuple-element.154, bf16[12,8,1,8,17,32]{5,3,4,1,0,2:T(8,128)(2,1)S(1)} %fusion.100), kind=kOutput, calls=%fused_computation.24.clone.1 | convolution fusion | flops 629686272 | bytes 2648064 | tf_op jit(solution)/shard_map/while/body/eval_jaxpr/conv_general_dilated | solution.py:56
  528.3 2.1 constant_dynamic-slice_fusion.2
  530.4 3.6 copy.61
  535.4 11.8 %fusion.100 = bf16[12,8,1,8,17,32]{5,3,4,1,0,2:T(8,128)(2,1)S(1)} fusion(pred[8,17]{0,1:T(8,128)(4,1)S(1)} %get-tuple-element.180, bf16[32,32,3,3,3]{1,0,4,3,2:T(8,128)(2,1)S(1)} %get-tuple-element.176, bf16[32,12,8,1,7,2]{0,4,5,2,1,3:T(8,128)(2,1)S(1)} %slice.90, bf16[32,12,8,1,8,17]{0,4,5,2,1,3:T(8,128)(2,1)S(1)} %copy.62), kind=kOutput, calls=%fused_computation.38.clone.1 | convolution fusion | flops 629489664 | bytes 1812616 | tf_op jit(solution)/shard_map/while/body/eval_jaxpr/conv_general_dilated | solution.py:56
  547.4 10.3 %fusion.102 = f32[12,8,8,17,32]{4,2,3,1,0:T(8,128)S(1)} fusion(bf16[32,32,3,3,3]{1,0,4,3,2:T(8,128)(2,1)S(1)} %copy-done.7, bf16[12,8,1,7,1,32]{5,3,4,1,0,2:T(8,128)(2,1)S(1)} %get-tuple-element.153, bf16[12,8,1,7,1,32]{5,3,4,1,0,2:T(8,128)(2,1)S(1)} %get-tuple-element.154, bf16[12,8,1,8,17,32]{5,3,4,1,0,2:T(8,128)(2,1)S(1)} %fusion.100), kind=kOutput, calls=%fused_computation.24.clone.1 | convolution fusion | flops 629686272 | bytes 2648064 | tf_op jit(solution)/shard_map/while/body/eval_jaxpr/conv_general_dilated | solution.py:56
  561.4 2.1 constant_dynamic-slice_fusion.2
  563.4 3.6 copy.61
  568.5 11.8 %fusion.100 = bf16[12,8,1,8,17,32]{5,3,4,1,0,2:T(8,128)(2,1)S(1)} fusion(pred[8,17]{0,1:T(8,128)(4,1)S(1)} %get-tuple-element.180, bf16[32,32,3,3,3]{1,0,4,3,2:T(8,128)(2,1)S(1)} %get-tuple-element.176, bf16[32,12,8,1,7,2]{0,4,5,2,1,3:T(8,128)(2,1)S(1)} %slice.90, bf16[32,12,8,1,8,17]{0,4,5,2,1,3:T(8,128)(2,1)S(1)} %copy.62), kind=kOutput, calls=%fused_computation.38.clone.1 | convolution fusion | flops 629489664 | bytes 1812616 | tf_op jit(solution)/shard_map/while/body/eval_jaxpr/conv_general_dilated | solution.py:56
  580.4 10.3 %fusion.102 = f32[12,8,8,17,32]{4,2,3,1,0:T(8,128)S(1)} fusion(bf16[32,32,3,3,3]{1,0,4,3,2:T(8,128)(2,1)S(1)} %copy-done.7, bf16[12,8,1,7,1,32]{5,3,4,1,0,2:T(8,128)(2,1)S(1)} %get-tuple-element.153, bf16[12,8,1,7,1,32]{5,3,4,1,0,2:T(8,128)(2,1)S(1)} %get-tuple-element.154, bf16[12,8,1,8,17,32]{5,3,4,1,0,2:T(8,128)(2,1)S(1)} %fusion.100), kind=kOutput, calls=%fused_computation.24.clone.1 | convolution fusion | flops 629686272 | bytes 2648064 | tf_op jit(solution)/shard_map/while/body/eval_jaxpr/conv_general_dilated | solution.py:56
  594.4 2.1 constant_dynamic-slice_fusion.2
  596.5 3.6 copy.61
  601.5 11.8 %fusion.100 = bf16[12,8,1,8,17,32]{5,3,4,1,0,2:T(8,128)(2,1)S(1)} fusion(pred[8,17]{0,1:T(8,128)(4,1)S(1)} %get-tuple-element.180, bf16[32,32,3,3,3]{1,0,4,3,2:T(8,128)(2,1)S(1)} %get-tuple-element.176, bf16[32,12,8,1,7,2]{0,4,5,2,1,3:T(8,128)(2,1)S(1)} %slice.90, bf16[32,12,8,1,8,17]{0,4,5,2,1,3:T(8,128)(2,1)S(1)} %copy.62), kind=kOutput, calls=%fused_computation.38.clone.1 | convolution fusion | flops 629489664 | bytes 1812616 | tf_op jit(solution)/shard_map/while/body/eval_jaxpr/conv_general_dilated | solution.py:56
  613.5 10.3 %fusion.102 = f32[12,8,8,17,32]{4,2,3,1,0:T(8,128)S(1)} fusion(bf16[32,32,3,3,3]{1,0,4,3,2:T(8,128)(2,1)S(1)} %copy-done.7, bf16[12,8,1,7,1,32]{5,3,4,1,0,2:T(8,128)(2,1)S(1)} %get-tuple-element.153, bf16[12,8,1,7,1,32]{5,3,4,1,0,2:T(8,128)(2,1)S(1)} %get-tuple-element.154, bf16[12,8,1,8,17,32]{5,3,4,1,0,2:T(8,128)(2,1)S(1)} %fusion.100), kind=kOutput, calls=%fused_computation.24.clone.1 | convolution fusion | flops 629686272 | bytes 2648064 | tf_op jit(solution)/shard_map/while/body/eval_jaxpr/conv_general_dilated | solution.py:56
  627.5 2.1 constant_dynamic-slice_fusion.2
  629.6 3.6 copy.61
  634.6 11.8 %fusion.100 = bf16[12,8,1,8,17,32]{5,3,4,1,0,2:T(8,128)(2,1)S(1)} fusion(pred[8,17]{0,1:T(8,128)(4,1)S(1)} %get-tuple-element.180, bf16[32,32,3,3,3]{1,0,4,3,2:T(8,128)(2,1)S(1)} %get-tuple-element.176, bf16[32,12,8,1,7,2]{0,4,5,2,1,3:T(8,128)(2,1)S(1)} %slice.90, bf16[32,12,8,1,8,17]{0,4,5,2,1,3:T(8,128)(2,1)S(1)} %copy.62), kind=kOutput, calls=%fused_computation.38.clone.1 | convolution fusion | flops 629489664 | bytes 1812616 | tf_op jit(solution)/shard_map/while/body/eval_jaxpr/conv_general_dilated | solution.py:56
  646.5 10.3 %fusion.102 = f32[12,8,8,17,32]{4,2,3,1,0:T(8,128)S(1)} fusion(bf16[32,32,3,3,3]{1,0,4,3,2:T(8,128)(2,1)S(1)} %copy-done.7, bf16[12,8,1,7,1,32]{5,3,4,1,0,2:T(8,128)(2,1)S(1)} %get-tuple-element.153, bf16[12,8,1,7,1,32]{5,3,4,1,0,2:T(8,128)(2,1)S(1)} %get-tuple-element.154, bf16[12,8,1,8,17,32]{5,3,4,1,0,2:T(8,128)(2,1)S(1)} %fusion.100), kind=kOutput, calls=%fused_computation.24.clone.1 | convolution fusion | flops 629686272 | bytes 2648064 | tf_op jit(solution)/shard_map/while/body/eval_jaxpr/conv_general_dilated | solution.py:56
  660.6 2.1 constant_dynamic-slice_fusion.2
  662.6 3.6 copy.61
  667.7 11.8 %fusion.100 = bf16[12,8,1,8,17,32]{5,3,4,1,0,2:T(8,128)(2,1)S(1)} fusion(pred[8,17]{0,1:T(8,128)(4,1)S(1)} %get-tuple-element.180, bf16[32,32,3,3,3]{1,0,4,3,2:T(8,128)(2,1)S(1)} %get-tuple-element.176, bf16[32,12,8,1,7,2]{0,4,5,2,1,3:T(8,128)(2,1)S(1)} %slice.90, bf16[32,12,8,1,8,17]{0,4,5,2,1,3:T(8,128)(2,1)S(1)} %copy.62), kind=kOutput, calls=%fused_computation.38.clone.1 | convolution fusion | flops 629489664 | bytes 1812616 | tf_op jit(solution)/shard_map/while/body/eval_jaxpr/conv_general_dilated | solution.py:56
  679.6 10.3 %fusion.102 = f32[12,8,8,17,32]{4,2,3,1,0:T(8,128)S(1)} fusion(bf16[32,32,3,3,3]{1,0,4,3,2:T(8,128)(2,1)S(1)} %copy-done.7, bf16[12,8,1,7,1,32]{5,3,4,1,0,2:T(8,128)(2,1)S(1)} %get-tuple-element.153, bf16[12,8,1,7,1,32]{5,3,4,1,0,2:T(8,128)(2,1)S(1)} %get-tuple-element.154, bf16[12,8,1,8,17,32]{5,3,4,1,0,2:T(8,128)(2,1)S(1)} %fusion.100), kind=kOutput, calls=%fused_computation.24.clone.1 | convolution fusion | flops 629686272 | bytes 2648064 | tf_op jit(solution)/shard_map/while/body/eval_jaxpr/conv_general_dilated | solution.py:56
  693.7 4.3 gather_fusion.5
  698.0 5.5 fusion.54
  703.5 54.6 %all-to-all-start.1 = ((f32[32,1,3,12,8,128]{5,4,3,2,1,0:T(8,128)}), f32[32,1,3,12,8,128]{5,4,3,2,1,0:T(8,128)}, u32[]{:S(2)}, u32[]{:S(2)}) async-start(f32[32,1,3,12,8,128]{5,4,3,2,1,0:T(8,128)} %fusion.54), calls=%async_computation.1 | async-start | bytes 9437184 | tf_op jit(solution)/shard_map/all_to_all | solution.py:155
  761.5 55.6 %all-to-all-done.1 = f32[32,1,3,12,8,128]{5,4,3,2,1,0:T(8,128)} async-done(((f32[32,1,3,12,8,128]{5,4,3,2,1,0:T(8,128)}), f32[32,1,3,12,8,128]{5,4,3,2,1,0:T(8,128)}, u32[]{:S(2)}, u32[]{:S(2)}) %all-to-all-start.1) | async-done | bytes 4718624 | tf_op jit(solution)/shard_map/all_to_all | solution.py:155
  817.1 3.0 gather_fusion.6
  820.7 3.7 collective-permute-start.2
  825.7 2.6 collective-permute-done.2
  828.3 4.1 collective-permute-done.3
  (138 shorter events, 45.7 us)
Async XLA Ops:
  0.0 10.7 %copy-start.9 = (u32[128]{0:T(128)S(1)}, u32[128]{0:T(128)}, u32[]{:S(2)}) copy-start(u32[128]{0:T(128)} %constant.243) | copy-start | bytes 1540
  0.0 11.3 %copy-start.1 = (s32[16]{0:T(128)S(1)}, s32[16]{0:T(128)}, u32[]{:S(2)}) copy-start(s32[16]{0:T(128)} %param.8) | copy-start | bytes 196
  5.4 49.1 %collective-permute-start = (bf16[16,32,2,8,128]{4,3,2,1,0:T(8,128)(2,1)}, bf16[16,32,2,8,128]{4,3,2,1,0:T(8,128)(2,1)S(1)}, u32[]{:S(2)}, u32[]{:S(2)}) collective-permute-start(bf16[16,32,2,8,128]{4,3,2,1,0:T(8,128)(2,1)} %get-tuple-element.103), channel_id=1, source_target_pairs={{0,1},{1,2},{2,3},{4,5},{5,6},{6,7},{8,9},{9,10},{10,11},{12,13},{... | collective-permute-start | bytes 6291464 | tf_op jit(solution)/shard_map/ppermute | solution.py:18
  9.4 49.4 %collective-permute-start.1 = (bf16[16,32,2,8,128]{4,3,2,1,0:T(8,128)(2,1)}, bf16[16,32,2,8,128]{4,3,2,1,0:T(8,128)(2,1)}, u32[]{:S(2)}, u32[]{:S(2)}) collective-permute-start(bf16[16,32,2,8,128]{4,3,2,1,0:T(8,128)(2,1)} %get-tuple-element.104), channel_id=1, source_target_pairs={{1,0},{2,1},{3,2},{5,4},{6,5},{7,6},{9,8},{10,9},{11,10},{13,12},{... | collective-permute-start | bytes 6291464 | tf_op jit(solution)/shard_map/ppermute | solution.py:20
  30.7 41.0 %copy-start.3 = (s32[16]{0:T(128)}, s32[16]{0:T(128)S(1)}, u32[]{:S(2)}) copy-start(s32[16]{0:T(128)S(1)} %reduce.2) | copy-start | bytes 196
  107.6 370.7 %all-to-all-start = ((bf16[32,1,32,12,8,128]{5,4,3,2,1,0:T(8,128)(2,1)}), bf16[32,1,32,12,8,128]{5,4,3,2,1,0:T(8,128)(2,1)}, u32[]{:S(2)}, u32[]{:S(2)}) async-start(bf16[32,1,32,12,8,128]{5,4,3,2,1,0:T(8,128)(2,1)} %fusion.52), calls=%async_computation | async-start | bytes 50331648 | tf_op jit(solution)/shard_map/all_to_all | solution.py:128
  489.9 5.1 copy-start.6
  489.9 5.1 copy-start.8
  489.9 5.1 copy-start.10
  502.4 11.9 %copy-start.7 = (bf16[32,32,3,3,3]{1,0,4,3,2:T(8,128)(2,1)S(1)}, bf16[32,32,3,3,3]{1,0,4,3,2:T(8,128)(2,1)}, u32[]{:S(2)}) copy-start(bf16[32,32,3,3,3]{1,0,4,3,2:T(8,128)(2,1)} %get-tuple-element.177) | copy-start | bytes 165892 | tf_op jit(solution)/shard_map/while
  535.4 11.9 %copy-start.7 = (bf16[32,32,3,3,3]{1,0,4,3,2:T(8,128)(2,1)S(1)}, bf16[32,32,3,3,3]{1,0,4,3,2:T(8,128)(2,1)}, u32[]{:S(2)}) copy-start(bf16[32,32,3,3,3]{1,0,4,3,2:T(8,128)(2,1)} %get-tuple-element.177) | copy-start | bytes 165892 | tf_op jit(solution)/shard_map/while
  568.5 11.9 %copy-start.7 = (bf16[32,32,3,3,3]{1,0,4,3,2:T(8,128)(2,1)S(1)}, bf16[32,32,3,3,3]{1,0,4,3,2:T(8,128)(2,1)}, u32[]{:S(2)}) copy-start(bf16[32,32,3,3,3]{1,0,4,3,2:T(8,128)(2,1)} %get-tuple-element.177) | copy-start | bytes 165892 | tf_op jit(solution)/shard_map/while
  601.5 11.9 %copy-start.7 = (bf16[32,32,3,3,3]{1,0,4,3,2:T(8,128)(2,1)S(1)}, bf16[32,32,3,3,3]{1,0,4,3,2:T(8,128)(2,1)}, u32[]{:S(2)}) copy-start(bf16[32,32,3,3,3]{1,0,4,3,2:T(8,128)(2,1)} %get-tuple-element.177) | copy-start | bytes 165892 | tf_op jit(solution)/shard_map/while
  634.6 11.9 %copy-start.7 = (bf16[32,32,3,3,3]{1,0,4,3,2:T(8,128)(2,1)S(1)}, bf16[32,32,3,3,3]{1,0,4,3,2:T(8,128)(2,1)}, u32[]{:S(2)}) copy-start(bf16[32,32,3,3,3]{1,0,4,3,2:T(8,128)(2,1)} %get-tuple-element.177) | copy-start | bytes 165892 | tf_op jit(solution)/shard_map/while
  667.7 11.9 %copy-start.7 = (bf16[32,32,3,3,3]{1,0,4,3,2:T(8,128)(2,1)S(1)}, bf16[32,32,3,3,3]{1,0,4,3,2:T(8,128)(2,1)}, u32[]{:S(2)}) copy-start(bf16[32,32,3,3,3]{1,0,4,3,2:T(8,128)(2,1)} %get-tuple-element.177) | copy-start | bytes 165892 | tf_op jit(solution)/shard_map/while
  693.7 4.3 copy-start
  693.7 4.3 copy-start.5
  703.5 56.7 %copy-start.2 = (s32[16]{0:T(128)S(1)}, s32[16]{0:T(128)}, u32[]{:S(2)}) copy-start(s32[16]{0:T(128)} %param.8) | copy-start | bytes 196
  703.5 56.7 %copy-start.4 = (s32[16]{0:T(128)S(1)}, s32[16]{0:T(128)}, u32[]{:S(2)}) copy-start(s32[16]{0:T(128)} %copy-done.3) | copy-start | bytes 196
  703.5 113.6 %all-to-all-start.1 = ((f32[32,1,3,12,8,128]{5,4,3,2,1,0:T(8,128)}), f32[32,1,3,12,8,128]{5,4,3,2,1,0:T(8,128)}, u32[]{:S(2)}, u32[]{:S(2)}) async-start(f32[32,1,3,12,8,128]{5,4,3,2,1,0:T(8,128)} %fusion.54), calls=%async_computation.1 | async-start | bytes 9437184 | tf_op jit(solution)/shard_map/all_to_all | solution.py:155
  820.7 7.6 collective-permute-start.2
  824.3 8.1 collective-permute-start.3
where the time goes:
time: 839 us; the launch traced here: 834 us
  waiting for transfers between devices  445 us (53%)
  matrix products  138 us (16%)
  local copies, waits for them, and re-layouts  99.3 us (12%)
  starting transfers between devices  72.7 us (9%)
  other arithmetic  60.3 us (7%)
  blocking collectives  16.9 us (2%)
    all_to_all x1, waiting for transfers between devices, on_device(): lax.all_to_all(outgoing.reshape((breadth, per_peer) + outgoing.shape[1:])...  358 us
    conv_general_dilated x12, matrix products, convolve(): lax.conv_general_dilated(inputs, kernel, (1, 1, 1), 'SAME', dimension_num...  133 us
    all_to_all x1, waiting for transfers between devices, on_device(): lax.all_to_all(backward.reshape((breadth, per_peer) + backward.shape[1:])...  55.6 us
    all_to_all x1, starting transfers between devices, on_device(): lax.all_to_all(backward.reshape((breadth, per_peer) + backward.shape[1:])...  54.6 us
    dynamic_slice x18, local copies, waits for them, and re-layouts, network(): return lax.map(single_block, blocks_in)  38.1 us
    ppermute x2, waiting for transfers between devices, padded_2(): lax.ppermute(tail, axis, [(i, (i + 1) % count) for i in range(ends)])  23.1 us
    select_n x1, other arithmetic, on_device(): jnp.where(present[:, None, None, None, None], outgoing, jnp.zeros((), out...  21.6 us
    unnamed x1, blocking collectives  16.9 us
  transfers between devices with their start and end apart: 6, of which 6 were waited for; matrix products, arithmetic and copies ran while one was open for 2% of the time, Pallas kernels for 0%

commit v1 on v0

v1 whole, which is shorter than its diff:
```python
import functools

import jax
import jax.numpy as jnp
from jax import lax
from jax.experimental import pallas as pl
from jax.experimental.pallas import tpu as pltpu
from jax.sharding import PartitionSpec as P

C = 32
AFF = 3
BLK = 16
BY = 8
BX = 128
ZD = 8
TZ = 12
ROWS = C * BY
TAPS = 3 * ROWS
BLEND = tuple(min(1.0, (t + 0.5) / 4, (TZ - t - 0.5) / 4) for t in range(TZ))
MESH = pl.DeviceIdType.MESH
f32 = jnp.float32
bf16 = jnp.bfloat16


def iota(shape, dim):
    return lax.broadcasted_iota(jnp.int32, shape, dim)


def put_shifted(planes, z, value, first, last):
    base = (z + 1) * TAPS
    value = value.astype(bf16)
    nothing = jnp.zeros_like(value)
    planes[base : base + ROWS, :] = jnp.where(first, nothing, pltpu.roll(value, 1, 1))
    planes[base + ROWS : base + 2 * ROWS, :] = value
    planes[base + 2 * ROWS : base + TAPS, :] = jnp.where(
        last, nothing, pltpu.roll(value, BX - 1, 1)
    )


def conv_pair(planes, weight, pair):
    base = 2 * pair * TAPS
    gathered = jnp.concatenate(
        [planes[base : base + 3 * TAPS, :], planes[base + TAPS : base + 4 * TAPS, :]], axis=1
    )
    return jnp.dot(weight[...], gathered, preferred_element_type=f32)


def tile_network(tile, acts_in, acts_mid, w_one, w_two, w_top, result, low, high):
    lane = iota((ROWS, BX), 1)
    first, last = lane == 0, lane == BX - 1
    sums, acts, logits = {}, {}, {}

    def prepare(p):
        value = tile[:, 16 * p : 16 * p + 16, :].astype(f32).reshape(C, 2, BY, BX)
        put_shifted(acts_in, 2 * p, value[:, 0].reshape(ROWS, BX), first, last)
        put_shifted(acts_in, 2 * p + 1, value[:, 1].reshape(ROWS, BX), first, last)

    def conv_one(p):
        sums[p] = conv_pair(acts_in, w_one, p)

    def relu_one(p):
        value = jnp.maximum(sums.pop(p), 0.0)
        put_shifted(acts_mid, 2 * p, value[:, :BX], first, last)
        put_shifted(acts_mid, 2 * p + 1, value[:, BX:], first, last)

    def conv_two(p):
        base = (2 * p + 1) * TAPS + ROWS
        own = jnp.concatenate(
            [acts_in[base : base + ROWS, :], acts_in[base + TAPS : base + TAPS + ROWS, :]], axis=1
        )
        value = conv_pair(acts_mid, w_two, p) + own.astype(f32)
        acts[p] = jnp.maximum(value, 0.0).astype(bf16)

    def head(p):
        value = jnp.dot(w_top[...], acts.pop(p), preferred_element_type=f32)
        pair = [value[:, :BX] * BLEND[2 * p], value[:, BX:] * BLEND[2 * p + 1]]
        if p == 0:
            low[...] = jnp.concatenate(pair, axis=0).astype(bf16)
        elif p == 5:
            high[...] = jnp.concatenate(pair, axis=0).astype(bf16)
        else:
            result[2 * p - 2] = pair[0]
            result[2 * p - 1] = pair[1]

    prepare(0)
    prepare(1)
    for p in range(9):
        if p < 6:
            conv_one(p)
        if p + 2 < 6:
            prepare(p + 2)
        if p < 6:
            relu_one(p)
        if 0 <= p - 2 < 6:
            conv_two(p - 2)
        if 0 <= p - 3 < 6:
            head(p - 3)


def build_banded(taps, banded):
    spread = (iota((C, ROWS), 1) // BY == iota((C, ROWS), 0)).astype(bf16)
    repeat = (iota((ROWS, C), 0) // BY == iota((ROWS, C), 1)).astype(bf16)
    apart = iota((ROWS, ROWS), 1) % BY - iota((ROWS, ROWS), 0) % BY
    for outer in range(9):
        total = jnp.zeros((ROWS, ROWS), f32)
        for dy in range(3):
            at = (outer * 3 + dy) * C
            wide = jnp.dot(taps[at : at + C, :], spread, preferred_element_type=f32).astype(bf16)
            wide = jnp.dot(repeat, wide, preferred_element_type=f32)
            total = jnp.where(apart == dy - 1, wide, total)
        banded[:, outer * ROWS : (outer + 1) * ROWS] = total.astype(bf16)


def build_head(w_head, banded):
    spread = (iota((C, ROWS), 1) // BY == iota((C, ROWS), 0)).astype(bf16)
    wide = jnp.dot(w_head[...], spread, preferred_element_type=f32)
    wide = jnp.broadcast_to(wide[:, None, :], (AFF, BY, ROWS)).reshape(AFF * BY, ROWS)
    apart = iota((AFF * BY, ROWS), 1) % BY - iota((AFF * BY, ROWS), 0) % BY
    banded[...] = jnp.where(apart == 0, wide, 0.0).astype(bf16)


def kernel(
    slots,
    occupied,
    features,
    taps_one,
    taps_two,
    w_head,
    out,
    held,
    tiles,
    acts_in,
    acts_mid,
    w_one,
    w_two,
    w_top,
    result,
    low,
    high,
    from_upper,
    from_lower,
    finished,
    load_sem,
    halo_send,
    halo_recv,
    edge_send,
    edge_recv,
):
    wide = lax.axis_index("wide")
    level = lax.axis_index("narrow")
    depth = 4
    above = (wide, lax.rem(level + 1, depth))
    below = (wide, lax.rem(level + depth - 1, depth))

    load = pltpu.make_async_copy(features, held, load_sem)
    load.start()
    barrier = pltpu.get_barrier_semaphore()
    for neighbour in (above, below):
        pl.semaphore_signal(barrier, inc=1, device_id=neighbour, device_id_type=MESH)
    pl.semaphore_wait(barrier, 2)

    running = []
    count = jnp.int32(0)
    for b in range(BLK):
        count = count + occupied[b]
        running.append(count)

    def halos(s):
        down = pltpu.make_async_remote_copy(
            src_ref=tiles.at[s, :, 16:32, :],
            dst_ref=tiles.at[s, :, 80:96, :],
            send_sem=halo_send.at[s, 0],
            recv_sem=halo_recv.at[s, 0],
            device_id=below,
            device_id_type=MESH,
        )
        up = pltpu.make_async_remote_copy(
            src_ref=tiles.at[s, :, 64:80, :],
            dst_ref=tiles.at[s, :, 0:16, :],
            send_sem=halo_send.at[s, 1],
            recv_sem=halo_recv.at[s, 1],
            device_id=above,
            device_id_type=MESH,
        )
        return down, up

    def edges(s):
        down = pltpu.make_async_remote_copy(
            src_ref=low.at[s],
            dst_ref=from_upper.at[s],
            send_sem=edge_send.at[s, 0],
            recv_sem=edge_recv.at[s, 0],
            device_id=below,
            device_id_type=MESH,
        )
        up = pltpu.make_async_remote_copy(
            src_ref=high.at[s],
            dst_ref=from_lower.at[s],
            send_sem=edge_send.at[s, 1],
            recv_sem=edge_recv.at[s, 1],
            device_id=above,
            device_id_type=MESH,
        )
        return down, up

    load.wait()

    @pl.loop(0, slots)
    def _(s):
        picked = jnp.int32(0)
        for b in range(BLK):
            picked = picked + (running[b] <= s).astype(jnp.int32)
        picked = jnp.minimum(picked, BLK - 1)
        tiles[s, :, 16:80, :] = held[picked]
        for copy in halos(s):
            copy.start()

    for planes in (acts_in, acts_mid):
        planes[0:TAPS, :] = jnp.zeros((TAPS, BX), bf16)
        planes[(TZ + 1) * TAPS : (TZ + 2) * TAPS, :] = jnp.zeros((TAPS, BX), bf16)
    build_banded(taps_one, w_one)
    build_banded(taps_two, w_two)
    build_head(w_head, w_top)

    @pl.loop(0, slots)
    def _(s):
        for copy in halos(s):
            copy.wait()

        @pl.when(level == 0)
        def _():
            tiles[s, :, 0:16, :] = jnp.zeros((C, 16, BX), bf16)

        @pl.when(level == depth - 1)
        def _():
            tiles[s, :, 80:96, :] = jnp.zeros((C, 16, BX), bf16)

        tile_network(
            tiles.at[s],
            acts_in,
            acts_mid,
            w_one,
            w_two,
            w_top,
            result.at[s],
            low.at[s],
            high.at[s],
        )
        for copy in edges(s):
            copy.start()

    has_lower, has_upper = level > 0, level < depth - 1

    @pl.loop(0, slots)
    def _(s):
        for copy in edges(s):
            copy.wait()
        planes = [result[s, z] for z in range(ZD)]
        lower = from_lower[s].astype(f32)
        upper = from_upper[s].astype(f32)
        for i in range(2):
            part = lower[24 * i : 24 * i + 24]
            planes[i] = jnp.where(has_lower, planes[i] + part, planes[i] / BLEND[2 + i])
            part = upper[24 * i : 24 * i + 24]
            planes[6 + i] = jnp.where(has_upper, planes[6 + i] + part, planes[6 + i] / BLEND[8 + i])
        for a in range(AFF):
            for p in range(4):
                two = [planes[2 * p + i][BY * a : BY * a + BY] for i in range(2)]
                finished[s, a, 16 * p : 16 * p + 16, :] = jnp.concatenate(two, axis=0).astype(bf16)

    for b in range(BLK):
        kept = finished[running[b] - occupied[b]]
        out[b] = jnp.where(occupied[b] > 0, kept, jnp.zeros_like(kept))


def on_device(features, occupied, w_first, w_second, w_head):
    slots = BLK
    stacked = jnp.stack([w_first, w_second])
    taps = jnp.transpose(stacked, (0, 3, 5, 4, 1, 2)).reshape(2, 27 * C, C)
    vmem = pl.BlockSpec(memory_space=pltpu.VMEM)
    call = pl.pallas_call(
        functools.partial(kernel, slots),
        out_shape=jax.ShapeDtypeStruct((BLK, AFF, ZD * BY, BX), bf16),
        in_specs=[
            pl.BlockSpec(memory_space=pltpu.SMEM),
            pl.BlockSpec(memory_space=pl.ANY),
            vmem,
            vmem,
            vmem,
        ],
        out_specs=vmem,
        scratch_shapes=[
            pltpu.VMEM((BLK, C, ZD * BY, BX), bf16),
            pltpu.VMEM((slots, C, TZ * BY, BX), bf16),
            pltpu.VMEM(((TZ + 2) * TAPS, BX), bf16),
            pltpu.VMEM(((TZ + 2) * TAPS, BX), bf16),
            pltpu.VMEM((ROWS, 9 * ROWS), bf16),
            pltpu.VMEM((ROWS, 9 * ROWS), bf16),
            pltpu.VMEM((AFF * BY, ROWS), bf16),
            pltpu.VMEM((slots, ZD, AFF * BY, BX), f32),
            pltpu.VMEM((slots, 2 * AFF * BY, BX), bf16),
            pltpu.VMEM((slots, 2 * AFF * BY, BX), bf16),
            pltpu.VMEM((slots, 2 * AFF * BY, BX), bf16),
            pltpu.VMEM((slots, 2 * AFF * BY, BX), bf16),
            pltpu.VMEM((slots, AFF, ZD * BY, BX), bf16),
            pltpu.SemaphoreType.DMA,
            pltpu.SemaphoreType.DMA((slots, 2)),
            pltpu.SemaphoreType.DMA((slots, 2)),
            pltpu.SemaphoreType.DMA((slots, 2)),
            pltpu.SemaphoreType.DMA((slots, 2)),
        ],
        compiler_params=pltpu.CompilerParams(
            collective_id=0, has_side_effects=True, vmem_limit_bytes=56 << 20
        ),
    )
    out = call(
        occupied, features.reshape(BLK, C, ZD * BY, BX), taps[0], taps[1], w_head
    )
    return out.reshape(BLK, AFF, ZD, BY, BX)


def solution(mesh):
    in_specs = (P("wide", None, "narrow", None, None), P("wide"), P(), P(), P())
    out_specs = P("wide", None, "narrow", None, None)
    return jax.shard_map(
        on_device, mesh=mesh, in_specs=in_specs, out_specs=out_specs, check_vma=False
    )
```

time: 839 us -> 96.9 us (0.12)
  waiting for transfers between devices: 445 us -> 0 us
  matrix products: 138 us -> 0 us
  local copies, waits for them, and re-layouts: 99.3 us -> 3.5 us
  Pallas kernels: 0 us -> 92.1 us
  starting transfers between devices: 72.7 us -> 0 us
  other arithmetic: 60.3 us -> 1.14 us
  blocking collectives: 16.9 us -> 0 us
    all_to_all x2 -> x0, waiting for transfers between devices: 413 us -> none  [the longest x1 358 us: on_device(): lax.all_to_all(outgoing.reshape((breadth, per_peer) + outgoing.shape[1:])...]
    conv_general_dilated x12 -> x0, matrix products: 133 us -> none  [convolve(): lax.conv_general_dilated(inputs, kernel, (1, 1, 1), 'SAME', dimension_num...]
    pallas_call x0 -> x1, Pallas kernels: none -> 92.1 us  [on_device(): call(occupied, features.reshape(BLK, C, ZD * BY, BX), taps[0], taps[1], w...]
    all_to_all x2 -> x0, starting transfers between devices: 62.4 us -> none  [the longest x1 54.6 us: on_device(): lax.all_to_all(backward.reshape((breadth, per_peer) + backward.shape[1:])...]
    dynamic_slice x19 -> x0, local copies, waits for them, and re-layouts: 38.7 us -> none  [the longest x18 38.1 us: network(): return lax.map(single_block, blocks_in)]
    gather x10 -> x0, local copies, waits for them, and re-layouts: 37.2 us -> none  [the longest x1 14.3 us: on_device(): outgoing = jnp.take(source, jnp.minimum(picked, home_slots - 1), axis=0)]
    select_n x9 -> x0, other arithmetic: 32.3 us -> none  [the longest x1 21.6 us: on_device(): jnp.where(present[:, None, None, None, None], outgoing, jnp.zeros((), out...]
    ppermute x4 -> x0, waiting for transfers between devices: 31.6 us -> none  [the longest x2 23.1 us: padded_2(): lax.ppermute(tail, axis, [(i, (i + 1) % count) for i in range(ends)])]
  transfers between devices with their start and end apart: 6 -> 0, of which waited for: 6 -> 0; matrix products, arithmetic and copies ran while one was open for 2% -> 0% of each run, Pallas kernels for 0% -> 0%
where the time goes in v1:
time: 96.9 us; the launch traced here: 96.7 us
  Pallas kernels  92.1 us (95%)
  local copies, waits for them, and re-layouts  3.5 us (4%)
  other arithmetic  1.14 us (1%)
    pallas_call x1, Pallas kernels, on_device(): call(occupied, features.reshape(BLK, C, ZD * BY, BX), taps[0], taps[1], w...  92.1 us
    unnamed x1, local copies, waits for them, and re-layouts  2.07 us

profile of v1, /device:TPU:0, one launch (start us, length us, event | category | flops | bytes accessed | tf_op | source)
XLA Modules:
  0.0 96.7 jit_solution(6703656040038807504)
XLA Ops:
  0.0 1.1 %maximum_bitcast_fusion = bf16[2,3,3,3,32,32]{5,4,2,3,1,0:T(8,128)(2,1)S(1)} fusion(bf16[1,32,32,3,3,3]{2,1,5,4,3,0:T(8,128)(2,1)} %bitcast.12, bf16[1,32,32,3,3,3]{2,1,5,4,3,0:T(8,128)(2,1)} %bitcast.13), kind=kLoop, calls=%fused_computation | loop fusion | flops 55296 | bytes 221184 | tf_op jit(solution)/shard_map/transpose | solution.py:279
  1.2 0.7 copy.7
  1.9 0.7 copy.6
  2.6 92.1 %shard_map.55 = bf16[16,3,64,128]{3,2,1,0:T(8,128)(2,1)} custom-call(s32[16]{0:T(128)} %occupied.1, bf16[16,32,64,128]{3,2,1,0:T(8,128)(2,1)} %bitcast.8, bf16[864,32]{1,0:T(8,128)(2,1)} %bitcast.11, bf16[864,32]{1,0:T(8,128)(2,1)} %bitcast.10, bf16[3,32]{1,0:T(4,128)(2,1)} %w_head.1), custom_call_target="tpu_custom_call" | custom-call | tf_op jit(solution)/shard_map/pallas_call | solution.py:316
  94.7 2.1 %copy.9 = bf16[16,3,8,8,128]{4,3,2,1,0:T(8,128)(2,1)} copy(bf16[16,3,8,8,128]{4,3,2,1,0:T(8,128)(2,1)} %bitcast.9) | data formatting | bytes 1572864
  (1 shorter events, 0.0 us)

commit v2 on v1

v2 whole, which is shorter than its diff:
```python
import functools

import jax
import jax.numpy as jnp
from jax import lax
from jax.experimental import pallas as pl
from jax.experimental.pallas import tpu as pltpu
from jax.sharding import PartitionSpec as P

C = 32
AFF = 3
BLK = 16
BY = 8
BX = 128
ZD = 8
TZ = 12
ROWS = C * BY
TAPS = 3 * ROWS
BLEND = tuple(min(1.0, (t + 0.5) / 4, (TZ - t - 0.5) / 4) for t in range(TZ))
MESH = pl.DeviceIdType.MESH
f32 = jnp.float32
bf16 = jnp.bfloat16


def iota(shape, dim):
    return lax.broadcasted_iota(jnp.int32, shape, dim)


def put_shifted(planes, z, value, first, last):
    base = (z + 1) * TAPS
    value = value.astype(bf16)
    nothing = jnp.zeros_like(value)
    planes[base : base + ROWS, :] = jnp.where(first, nothing, pltpu.roll(value, 1, 1))
    planes[base + ROWS : base + 2 * ROWS, :] = value
    planes[base + 2 * ROWS : base + TAPS, :] = jnp.where(
        last, nothing, pltpu.roll(value, BX - 1, 1)
    )


def conv_pair(planes, weight, pair):
    base = 2 * pair * TAPS
    gathered = jnp.concatenate(
        [planes[base : base + 3 * TAPS, :], planes[base + TAPS : base + 4 * TAPS, :]], axis=1
    )
    return jnp.dot(weight[...], gathered, preferred_element_type=f32)


def tile_network(tile, acts_in, acts_mid, w_one, w_two, w_top, result, low, high):
    lane = iota((ROWS, BX), 1)
    first, last = lane == 0, lane == BX - 1
    sums, acts, logits = {}, {}, {}

    def prepare(p):
        value = tile[:, 16 * p : 16 * p + 16, :].astype(f32).reshape(C, 2, BY, BX)
        put_shifted(acts_in, 2 * p, value[:, 0].reshape(ROWS, BX), first, last)
        put_shifted(acts_in, 2 * p + 1, value[:, 1].reshape(ROWS, BX), first, last)

    def conv_one(p):
        sums[p] = conv_pair(acts_in, w_one, p)

    def relu_one(p):
        value = jnp.maximum(sums.pop(p), 0.0)
        put_shifted(acts_mid, 2 * p, value[:, :BX], first, last)
        put_shifted(acts_mid, 2 * p + 1, value[:, BX:], first, last)

    def conv_two(p):
        base = (2 * p + 1) * TAPS + ROWS
        own = jnp.concatenate(
            [acts_in[base : base + ROWS, :], acts_in[base + TAPS : base + TAPS + ROWS, :]], axis=1
        )
        value = conv_pair(acts_mid, w_two, p) + own.astype(f32)
        acts[p] = jnp.maximum(value, 0.0).astype(bf16)

    def head(p):
        value = jnp.dot(w_top[...], acts.pop(p), preferred_element_type=f32)
        pair = [value[:, :BX] * BLEND[2 * p], value[:, BX:] * BLEND[2 * p + 1]]
        if p == 0:
            low[...] = jnp.concatenate(pair, axis=0).astype(bf16)
        elif p == 5:
            high[...] = jnp.concatenate(pair, axis=0).astype(bf16)
        else:
            result[2 * p - 2] = pair[0]
            result[2 * p - 1] = pair[1]

    prepare(0)
    prepare(1)
    for p in range(9):
        if p < 6:
            conv_one(p)
        if p + 2 < 6:
            prepare(p + 2)
        if p < 6:
            relu_one(p)
        if 0 <= p - 2 < 6:
            conv_two(p - 2)
        if 0 <= p - 3 < 6:
            head(p - 3)


def build_banded(taps, banded):
    spread = (iota((C, ROWS), 1) // BY == iota((C, ROWS), 0)).astype(bf16)
    repeat = (iota((ROWS, C), 0) // BY == iota((ROWS, C), 1)).astype(bf16)
    apart = iota((ROWS, ROWS), 1) % BY - iota((ROWS, ROWS), 0) % BY
    for outer in range(9):
        total = jnp.zeros((ROWS, ROWS), f32)
        for dy in range(3):
            at = ((outer // 3 * 3 + dy) * 3 + outer % 3) * C
            wide = jnp.dot(taps[at : at + C, :], spread, preferred_element_type=f32).astype(bf16)
            wide = jnp.dot(repeat, wide, preferred_element_type=f32)
            total = jnp.where(apart == dy - 1, wide, total)
        banded[:, outer * ROWS : (outer + 1) * ROWS] = total.astype(bf16)


def build_head(w_head, banded):
    spread = (iota((C, ROWS), 1) // BY == iota((C, ROWS), 0)).astype(bf16)
    wide = jnp.dot(w_head[...], spread, preferred_element_type=f32)
    wide = jnp.broadcast_to(wide[:, None, :], (AFF, BY, ROWS)).reshape(AFF * BY, ROWS)
    apart = iota((AFF * BY, ROWS), 1) % BY - iota((AFF * BY, ROWS), 0) % BY
    banded[...] = jnp.where(apart == 0, wide, 0.0).astype(bf16)


DEPTH = 4


def running_counts(occupied):
    running = []
    count = jnp.int32(0)
    for b in range(BLK):
        count = count + occupied[b]
        running.append(count)
    return running


def block_of_rank(running, rank):
    picked = jnp.int32(0)
    for b in range(BLK):
        picked = picked + jnp.where(running[b] <= rank, 1, 0)
    return jnp.minimum(picked, BLK - 1)


def halo_copies(tiles, send, recv, above, below, s):
    down = pltpu.make_async_remote_copy(
        src_ref=tiles.at[s, :, 16:32, :],
        dst_ref=tiles.at[s, :, 80:96, :],
        send_sem=send.at[s, 0],
        recv_sem=recv.at[s, 0],
        device_id=below,
        device_id_type=MESH,
    )
    up = pltpu.make_async_remote_copy(
        src_ref=tiles.at[s, :, 64:80, :],
        dst_ref=tiles.at[s, :, 0:16, :],
        send_sem=send.at[s, 1],
        recv_sem=recv.at[s, 1],
        device_id=above,
        device_id_type=MESH,
    )
    return down, up


def edge_copies(low, high, from_upper, from_lower, send, recv, above, below, s):
    down = pltpu.make_async_remote_copy(
        src_ref=low.at[s],
        dst_ref=from_upper.at[s],
        send_sem=send.at[s, 0],
        recv_sem=recv.at[s, 0],
        device_id=below,
        device_id_type=MESH,
    )
    up = pltpu.make_async_remote_copy(
        src_ref=high.at[s],
        dst_ref=from_lower.at[s],
        send_sem=send.at[s, 1],
        recv_sem=recv.at[s, 1],
        device_id=above,
        device_id_type=MESH,
    )
    return down, up


def clear_outside(tiles, s, level):
    @pl.when(level == 0)
    def _():
        tiles[s, :, 0:16, :] = jnp.zeros((C, 16, BX), bf16)

    @pl.when(level == DEPTH - 1)
    def _():
        tiles[s, :, 80:96, :] = jnp.zeros((C, 16, BX), bf16)


def finish(result, from_lower, from_upper, finished, s, level):
    has_lower, has_upper = level > 0, level < DEPTH - 1
    planes = [result[s, z] for z in range(ZD)]
    lower = from_lower[s].astype(f32)
    upper = from_upper[s].astype(f32)
    for i in range(2):
        part = lower[24 * i : 24 * i + 24]
        planes[i] = jnp.where(has_lower, planes[i] + part, planes[i] / BLEND[2 + i])
        part = upper[24 * i : 24 * i + 24]
        planes[6 + i] = jnp.where(has_upper, planes[6 + i] + part, planes[6 + i] / BLEND[8 + i])
    for a in range(AFF):
        for p in range(4):
            two = [planes[2 * p + i][BY * a : BY * a + BY] for i in range(2)]
            finished[s, a, 16 * p : 16 * p + 16, :] = jnp.concatenate(two, axis=0).astype(bf16)


def whole_kernel(
    slots,
    occupied,
    features,
    taps_one,
    taps_two,
    w_head,
    out,
    held,
    tiles,
    acts_in,
    acts_mid,
    w_one,
    w_two,
    w_top,
    result,
    low,
    high,
    from_upper,
    from_lower,
    finished,
    load_sem,
    halo_send,
    halo_recv,
    edge_send,
    edge_recv,
):
    wide = lax.axis_index("wide")
    level = lax.axis_index("narrow")
    above = (wide, lax.rem(level + 1, DEPTH))
    below = (wide, lax.rem(level + DEPTH - 1, DEPTH))

    load = pltpu.make_async_copy(features, held, load_sem)
    load.start()
    barrier = pltpu.get_barrier_semaphore()
    for neighbour in (above, below):
        pl.semaphore_signal(barrier, inc=1, device_id=neighbour, device_id_type=MESH)
    pl.semaphore_wait(barrier, 2)

    running = running_counts(occupied)
    halos = functools.partial(halo_copies, tiles, halo_send, halo_recv, above, below)
    edges = functools.partial(
        edge_copies, low, high, from_upper, from_lower, edge_send, edge_recv, above, below
    )
    load.wait()

    @pl.loop(0, slots)
    def _(s):
        tiles[s, :, 16:80, :] = held[block_of_rank(running, s)]
        for copy in halos(s):
            copy.start()

    for planes in (acts_in, acts_mid):
        planes[0:TAPS, :] = jnp.zeros((TAPS, BX), bf16)
        planes[(TZ + 1) * TAPS : (TZ + 2) * TAPS, :] = jnp.zeros((TAPS, BX), bf16)
    build_banded(taps_one, w_one)
    build_banded(taps_two, w_two)
    build_head(w_head, w_top)

    @pl.loop(0, slots)
    def _(s):
        for copy in halos(s):
            copy.wait()
        clear_outside(tiles, s, level)
        tile_network(
            tiles.at[s],
            acts_in,
            acts_mid,
            w_one,
            w_two,
            w_top,
            result.at[s],
            low.at[s],
            high.at[s],
        )
        for copy in edges(s):
            copy.start()

    @pl.loop(0, slots)
    def _(s):
        for copy in edges(s):
            copy.wait()
        finish(result, from_lower, from_upper, finished, s, level)

    for b in range(BLK):
        kept = finished[running[b] - occupied[b]]
        out[b] = jnp.where(occupied[b] > 0, kept, jnp.zeros_like(kept))


SLOTS = 7
SURE = 3
LATE = 5
TARGET = 5
TWINS = 3
EARLY = TWINS + 4
LANES = EARLY + 2
COLUMNS = 32


def lane_columns(lane, sign):
    column = lax.axis_index("wide")
    core, y, x = column % 2, column // 2 % 4, column // 8
    if lane < TWINS:
        return column + 1 - 2 * core
    if lane < EARLY:
        step = sign * (1, -1, 1, -1)[lane - TWINS] + 4
        if lane < TWINS + 2:
            x = (x + step) % 4
        else:
            y = (y + step) % 4
        return (x * 4 + y) * 2 + core
    step = sign * (1, -1)[lane - EARLY]
    along_x = 1 - core if sign > 0 else core
    x = (x + step * along_x + 4) % 4
    y = (y + step * (1 - along_x) + 4) % 4
    return (x * 4 + y) * 2 + 1 - core


def turned(value, dim, step):
    step = step % 4
    if step == 0:
        return value
    head = lax.slice_in_dim(value, 0, step, axis=dim)
    return jnp.concatenate([lax.slice_in_dim(value, step, 4, axis=dim), head], axis=dim)


def other_core(value):
    return jnp.concatenate([value[:, :, 1:2], value[:, :, 0:1]], axis=2)


def across(value, lane, sign):
    if lane < TWINS:
        return other_core(value)
    if lane < EARLY:
        step = sign * (1, -1, 1, -1)[lane - TWINS]
        return turned(value, 0 if lane < TWINS + 2 else 1, step)
    step = sign * (1, -1)[lane - EARLY]
    flipped = other_core(value)
    over_x, over_y = turned(flipped, 0, step), turned(flipped, 1, step)
    pair = (over_x, over_y) if sign > 0 else (over_y, over_x)
    return jnp.concatenate([pair[0][:, :, 0:1], pair[1][:, :, 1:2]], axis=2)


def make_plan(counts, used):
    load = counts
    own = counts
    for turn in range(3):
        for lane in range(LANES):
            there = across(load, lane, 1)
            sends = (load > TARGET) & (load - there >= 2) & (own > 0)
            if turn == 0:
                sends = sends & (there < TARGET)
            else:
                sends = sends & (used[lane].reshape(load.shape) == 0)
            sends = jnp.where(sends, 1, 0)
            if turn == 0:
                used[lane] = sends.reshape(used.shape[1:])
            else:
                used[lane] = used[lane] + sends.reshape(used.shape[1:])
            own = own - sends
            load = load - sends + across(sends, lane, -1)
    early = jnp.zeros_like(load)
    late = jnp.zeros_like(load)
    for lane in range(LANES):
        taken = across(used[lane].reshape(load.shape), lane, -1)
        if lane < EARLY:
            early = early + taken
        else:
            late = late + taken
    need = jnp.maximum(own, SURE) + early
    need = jnp.where(late > 0, jnp.maximum(need, LATE) + late, need)
    return jnp.max(need.reshape((COLUMNS,) + need.shape[3:]), axis=0)


def shared_kernel(
    occupied,
    features,
    taps_one,
    taps_two,
    w_head,
    out,
    needed,
    held,
    tiles,
    acts_in,
    acts_mid,
    w_one,
    w_two,
    w_top,
    result,
    low,
    high,
    from_upper,
    from_lower,
    finished,
    mine,
    counts,
    used,
    early_out,
    early_in,
    late_out,
    late_in,
    back_out,
    back_in,
    load_sem,
    count_send,
    count_recv,
    lane_send,
    lane_recv,
    back_send,
    back_recv,
    halo_send,
    halo_recv,
    edge_send,
    edge_recv,
):
    wide = lax.axis_index("wide")
    level = lax.axis_index("narrow")
    above = (wide, lax.rem(level + 1, DEPTH))
    below = (wide, lax.rem(level + DEPTH - 1, DEPTH))

    load = pltpu.make_async_copy(features, held, load_sem)
    load.start()
    barrier = pltpu.get_barrier_semaphore()
    for neighbour in (above, below):
        pl.semaphore_signal(barrier, inc=1, device_id=neighbour, device_id_type=MESH)

    @pl.loop(1, COLUMNS)
    def _(o):
        pl.semaphore_signal(
            barrier,
            inc=1,
            device_id=(lax.rem(wide + o, COLUMNS), level),
            device_id_type=MESH,
        )

    running = running_counts(occupied)
    held_blocks = running[-1]
    mine[...] = jnp.full(mine.shape, held_blocks, jnp.int32)
    counts[wide] = mine[...]
    pl.semaphore_wait(barrier, COLUMNS + 1)

    def count_copy(o):
        return pltpu.make_async_remote_copy(
            src_ref=mine,
            dst_ref=counts.at[wide],
            send_sem=count_send.at[o],
            recv_sem=count_recv.at[o],
            device_id=(lax.rem(wide + o, COLUMNS), level),
            device_id_type=MESH,
        )

    @pl.loop(1, COLUMNS)
    def _(o):
        count_copy(o).start()

    def lane_copy(lane):
        if lane < EARLY:
            source, target = early_out.at[lane], early_in.at[lane]
        else:
            source, target = late_out.at[lane - EARLY], late_in.at[lane - EARLY]
        return pltpu.make_async_remote_copy(
            src_ref=source,
            dst_ref=target,
            send_sem=lane_send.at[lane],
            recv_sem=lane_recv.at[lane],
            device_id=(lane_columns(lane, 1), level),
            device_id_type=MESH,
        )

    def back_copy(lane):
        return pltpu.make_async_remote_copy(
            src_ref=back_out.at[lane],
            dst_ref=back_in.at[lane],
            send_sem=back_send.at[lane],
            recv_sem=back_recv.at[lane],
            device_id=(lane_columns(lane, -1), level),
            device_id_type=MESH,
        )

    halos = functools.partial(halo_copies, tiles, halo_send, halo_recv, above, below)
    edges = functools.partial(
        edge_copies, low, high, from_upper, from_lower, edge_send, edge_recv, above, below
    )

    build_banded(taps_one, w_one)
    load.wait()
    for s in range(SURE):
        tiles[s, :, 16:80, :] = held[block_of_rank(running, s)]
        for copy in halos(s):
            copy.start()

    @pl.loop(1, COLUMNS)
    def _(o):
        count_copy(o).wait()

    tile_shape = (4, 4, 2) + counts.shape[1:]
    needed[...] = make_plan(counts[...].reshape(tile_shape), used)

    sent, taken = [], []
    for lane in range(LANES):
        sent.append(used[lane, wide, 0, 0])
        taken.append(used[lane, lane_columns(lane, -1), 0, 0])
    kept = held_blocks - sum(sent)
    ranks = []
    rank = kept
    for lane in range(LANES):
        ranks.append(rank)
        rank = rank + sent[lane]
    places = []
    place = jnp.maximum(kept, SURE)
    for lane in range(LANES):
        if lane == EARLY:
            place = jnp.maximum(place, LATE)
        places.append(place)
        place = place + taken[lane]

    for lane in range(EARLY):
        early_out[lane] = held[block_of_rank(running, ranks[lane])]
        lane_copy(lane).start()

    for planes in (acts_in, acts_mid):
        planes[0:TAPS, :] = jnp.zeros((TAPS, BX), bf16)
        planes[(TZ + 1) * TAPS : (TZ + 2) * TAPS, :] = jnp.zeros((TAPS, BX), bf16)
    build_banded(taps_two, w_two)
    build_head(w_head, w_top)

    def stage(s):
        own = held[block_of_rank(running, s)]
        chosen = jnp.int32(0)
        for lane in range(EARLY):
            chosen = chosen + jnp.where((taken[lane] > 0) & (places[lane] == s), lane, 0)
        value = jnp.where(s < kept, own, early_in[chosen])
        if s >= LATE:
            chosen, found = jnp.int32(0), jnp.int32(0)
            for lane in range(EARLY, LANES):
                here = (taken[lane] > 0) & (places[lane] == s)
                chosen = chosen + jnp.where(here, lane - EARLY, 0)
                found = found + jnp.where(here, 1, 0)
            value = jnp.where(found > 0, late_in[chosen], value)
        tiles[s, :, 16:80, :] = value
        for copy in halos(s):
            copy.start()

    @pl.loop(0, SLOTS)
    def _(s):
        @pl.when(s == 1)
        def _():
            for lane in range(EARLY, LANES):
                late_out[lane - EARLY] = held[block_of_rank(running, ranks[lane])]
                lane_copy(lane).start()

        @pl.when(s == SURE - 1)
        def _():
            for lane in range(EARLY):
                lane_copy(lane).wait()
            for later in range(SURE, LATE):
                stage(later)

        @pl.when(s == LATE - 1)
        def _():
            for lane in range(EARLY, LANES):
                lane_copy(lane).wait()
            for later in range(LATE, SLOTS):
                stage(later)

        for copy in halos(s):
            copy.wait()
        clear_outside(tiles, s, level)
        tile_network(
            tiles.at[s],
            acts_in,
            acts_mid,
            w_one,
            w_two,
            w_top,
            result.at[s],
            low.at[s],
            high.at[s],
        )
        for copy in edges(s):
            copy.start()

    @pl.loop(0, SLOTS)
    def _(s):
        for copy in edges(s):
            copy.wait()
        finish(result, from_lower, from_upper, finished, s, level)

    for lane in range(LANES):
        back_out[lane] = finished[jnp.clip(places[lane], 0, SLOTS - 1)]
        back_copy(lane).start()
    for lane in range(LANES):
        back_copy(lane).wait()

    for b in range(BLK):
        rank = running[b] - occupied[b]
        chosen = jnp.int32(0)
        for lane in range(LANES):
            chosen = chosen + jnp.where((sent[lane] > 0) & (ranks[lane] == rank), lane, 0)
        local = finished[jnp.minimum(rank, SLOTS - 1)]
        value = jnp.where(rank < kept, local, back_in[chosen])
        out[b] = jnp.where(occupied[b] > 0, value, jnp.zeros_like(value))


def work_scratch(slots):
    return [
        pltpu.VMEM((BLK, C, ZD * BY, BX), bf16),
        pltpu.VMEM((slots, C, TZ * BY, BX), bf16),
        pltpu.VMEM(((TZ + 2) * TAPS, BX), bf16),
        pltpu.VMEM(((TZ + 2) * TAPS, BX), bf16),
        pltpu.VMEM((ROWS, 9 * ROWS), bf16),
        pltpu.VMEM((ROWS, 9 * ROWS), bf16),
        pltpu.VMEM((AFF * BY, ROWS), bf16),
        pltpu.VMEM((slots, ZD, AFF * BY, BX), f32),
        pltpu.VMEM((slots, 2 * AFF * BY, BX), bf16),
        pltpu.VMEM((slots, 2 * AFF * BY, BX), bf16),
        pltpu.VMEM((slots, 2 * AFF * BY, BX), bf16),
        pltpu.VMEM((slots, 2 * AFF * BY, BX), bf16),
        pltpu.VMEM((slots, AFF, ZD * BY, BX), bf16),
    ]


def on_device(features, occupied, w_first, w_second, w_head):
    vmem = pl.BlockSpec(memory_space=pltpu.VMEM)
    in_specs = [
        pl.BlockSpec(memory_space=pltpu.SMEM),
        pl.BlockSpec(memory_space=pl.ANY),
        vmem,
        vmem,
        vmem,
    ]
    affinities = jax.ShapeDtypeStruct((BLK, AFF, ZD * BY, BX), bf16)
    dma = pltpu.SemaphoreType.DMA
    shared = pl.pallas_call(
        shared_kernel,
        out_shape=[affinities, jax.ShapeDtypeStruct((8, 128), jnp.int32)],
        in_specs=in_specs,
        out_specs=[vmem, vmem],
        scratch_shapes=work_scratch(SLOTS)
        + [
            pltpu.VMEM((8, 128), jnp.int32),
            pltpu.VMEM((COLUMNS, 8, 128), jnp.int32),
            pltpu.VMEM((LANES, COLUMNS, 8, 128), jnp.int32),
            pltpu.VMEM((EARLY, C, ZD * BY, BX), bf16),
            pltpu.VMEM((EARLY, C, ZD * BY, BX), bf16),
            pltpu.VMEM((LANES - EARLY, C, ZD * BY, BX), bf16),
            pltpu.VMEM((LANES - EARLY, C, ZD * BY, BX), bf16),
            pltpu.VMEM((LANES, AFF, ZD * BY, BX), bf16),
            pltpu.VMEM((LANES, AFF, ZD * BY, BX), bf16),
            dma,
            dma((COLUMNS,)),
            dma((COLUMNS,)),
            dma((LANES,)),
            dma((LANES,)),
            dma((LANES,)),
            dma((LANES,)),
            dma((SLOTS, 2)),
            dma((SLOTS, 2)),
            dma((SLOTS, 2)),
            dma((SLOTS, 2)),
        ],
        compiler_params=pltpu.CompilerParams(
            collective_id=0, has_side_effects=True, vmem_limit_bytes=56 << 20
        ),
    )
    whole = pl.pallas_call(
        functools.partial(whole_kernel, BLK),
        out_shape=affinities,
        in_specs=in_specs,
        out_specs=vmem,
        scratch_shapes=work_scratch(BLK)
        + [dma, dma((BLK, 2)), dma((BLK, 2)), dma((BLK, 2)), dma((BLK, 2))],
        compiler_params=pltpu.CompilerParams(
            collective_id=1, has_side_effects=True, vmem_limit_bytes=56 << 20
        ),
    )
    taps = [
        jnp.transpose(w, (2, 3, 4, 0, 1)).reshape(27 * C, C) for w in (w_first, w_second)
    ]
    args = (occupied, features.reshape(BLK, C, ZD * BY, BX), *taps, w_head)
    out, needed = shared(*args)
    out = lax.cond(needed[0, 0] > SLOTS, lambda: whole(*args), lambda: out)
    return out.reshape(BLK, AFF, ZD, BY, BX)


def solution(mesh):
    in_specs = (P("wide", None, "narrow", None, None), P("wide"), P(), P(), P())
    out_specs = P("wide", None, "narrow", None, None)
    return jax.shard_map(
        on_device, mesh=mesh, in_specs=in_specs, out_specs=out_specs, check_vma=False
    )
```

time: 96.9 us -> 69.7 us (0.72); the launches traced: 96.7 us -> 68.6 us
  Pallas kernels: 92.1 us -> 65.8 us
  local copies, waits for them, and re-layouts: 3.5 us -> 2.09 us
  other arithmetic: 1.14 us -> 0 us
    pallas_call x1, Pallas kernels: 92.1 us -> 65.8 us  [on_device(): out, needed = shared(*args)]
    unnamed x1 -> x9, local copies, waits for them, and re-layouts: 2.07 us -> 0.9 us
    transpose x1 -> x0, other arithmetic: 1.14 us -> none  [on_device(): taps = jnp.transpose(stacked, (0, 3, 5, 4, 1, 2)).reshape(2, 27 * C, C)]
where the time goes in v2:
time: 69.7 us; the launch traced here: 68.6 us
  Pallas kernels  65.8 us (94%)
  local copies, waits for them, and re-layouts  2.09 us (3%)
  between operations  0.7 us (1%)
    pallas_call x1, Pallas kernels, on_device(): out, needed = shared(*args)  65.8 us

profile of v2, /device:TPU:0, one launch (start us, length us, event | category | flops | bytes accessed | tf_op | source)
XLA Modules:
  0.0 68.6 jit_solution(2813543542125248757)
XLA Ops:
  0.0 0.0 copy-start.2
  0.0 0.0 copy-start.3
  0.0 0.0 copy-start.1
  0.0 0.0 copy-start
  0.0 65.8 %shard_map.57 = (bf16[16,3,64,128]{3,2,1,0:T(8,128)(2,1)S(1)}, s32[8,128]{1,0:T(8,128)}) custom-call(s32[16]{0:T(128)} %occupied.1, bf16[16,32,64,128]{3,2,1,0:T(8,128)(2,1)} %bitcast.10, bf16[864,32]{1,0:T(8,128)(2,1)} %bitcast.12, bf16[864,32]{1,0:T(8,128)(2,1)} %bitcast.14, bf16[3,32]{1,0:T(4,128)(2,1)} %w_head.1), custom_call_target="tpu_custom_call" | custom-call | tf_op jit(solution)/shard_map/pallas_call | solution.py:688
  65.8 1.2 %slice.3 = s32[1,1]{1,0:T(1,128)} slice(s32[8,128]{1,0:T(8,128)} %get-tuple-element.28), slice={[0:1], [0:1]} | slice | bytes 8 | tf_op jit(solution)/shard_map/slice | solution.py:689
  67.6 0.0 copy-done.2
  67.6 0.0 copy-done.3
  67.6 0.0 copy-done.1
  67.7 0.0 copy-done
  67.7 0.9 %copy.12 = bf16[16,3,8,8,128]{4,3,2,1,0:T(8,128)(2,1)} copy(bf16[16,3,8,8,128]{4,3,2,1,0:T(8,128)(2,1)S(1)} %get-tuple-element.30) | data formatting | bytes 1572864
  (1 shorter events, 0.0 us)
Async XLA Ops:
  0.0 67.6 %copy-start.2 = (bf16[3,32]{1,0:T(4,128)(2,1)S(1)}, bf16[3,32]{1,0:T(4,128)(2,1)}, u32[]{:S(2)}) copy-start(bf16[3,32]{1,0:T(4,128)(2,1)} %w_head.1) | copy-start | bytes 580
  0.0 67.6 %copy-start.3 = (s32[16]{0:T(128)S(1)}, s32[16]{0:T(128)}, u32[]{:S(2)}) copy-start(s32[16]{0:T(128)} %occupied.1) | copy-start | bytes 196
  0.0 67.6 %copy-start.1 = (bf16[32,32,3,3,3]{1,0,4,3,2:T(8,128)(2,1)S(1)}, bf16[32,32,3,3,3]{1,0,4,3,2:T(8,128)(2,1)}, u32[]{:S(2)}) copy-start(bf16[32,32,3,3,3]{1,0,4,3,2:T(8,128)(2,1)} %param.10) | copy-start | bytes 165892
  0.0 67.7 %copy-start = (bf16[32,32,3,3,3]{1,0,4,3,2:T(8,128)(2,1)S(1)}, bf16[32,32,3,3,3]{1,0,4,3,2:T(8,128)(2,1)}, u32[]{:S(2)}) copy-start(bf16[32,32,3,3,3]{1,0,4,3,2:T(8,128)(2,1)} %param.9) | copy-start | bytes 165892

commit v3 on v2

v3 whole, which is shorter than its diff:
```python
import functools

import jax
import jax.numpy as jnp
from jax import lax
from jax.experimental import pallas as pl
from jax.experimental.pallas import tpu as pltpu
from jax.sharding import PartitionSpec as P

C = 32
AFF = 3
BLK = 16
BY = 8
BX = 128
ZD = 8
TZ = 12
ROWS = C * BY
TAPS = 3 * ROWS
BLEND = tuple(min(1.0, (t + 0.5) / 4, (TZ - t - 0.5) / 4) for t in range(TZ))
MESH = pl.DeviceIdType.MESH
f32 = jnp.float32
bf16 = jnp.bfloat16


def iota(shape, dim):
    return lax.broadcasted_iota(jnp.int32, shape, dim)


def put_shifted(planes, z, value, first, last):
    base = (z + 1) * TAPS
    value = value.astype(bf16)
    nothing = jnp.zeros_like(value)
    planes[base : base + ROWS, :] = jnp.where(first, nothing, pltpu.roll(value, 1, 1))
    planes[base + ROWS : base + 2 * ROWS, :] = value
    planes[base + 2 * ROWS : base + TAPS, :] = jnp.where(
        last, nothing, pltpu.roll(value, BX - 1, 1)
    )


def conv_pair(planes, weight, pair):
    base = 2 * pair * TAPS
    gathered = jnp.concatenate(
        [planes[base : base + 3 * TAPS, :], planes[base + TAPS : base + 4 * TAPS, :]], axis=1
    )
    return jnp.dot(weight[...], gathered, preferred_element_type=f32)


def work_through(
    slots,
    level,
    tiles,
    acts_in,
    acts_mid,
    w_one,
    w_two,
    w_top,
    result,
    low,
    high,
    finished,
    from_lower,
    from_upper,
    halos,
    edges,
    before,
):
    lane = iota((ROWS, BX), 1)
    first, last = lane == 0, lane == BX - 1

    def prepare(s, p):
        value = tiles[s, :, 16 * p : 16 * p + 16, :].astype(f32)
        if p == 0:
            value = jnp.where(level > 0, value, 0.0)
        if p == 5:
            value = jnp.where(level < DEPTH - 1, value, 0.0)
        value = value.reshape(C, 2, BY, BX)
        put_shifted(acts_in, 2 * p, value[:, 0].reshape(ROWS, BX), first, last)
        put_shifted(acts_in, 2 * p + 1, value[:, 1].reshape(ROWS, BX), first, last)

    def conv_one(p):
        value = jnp.maximum(conv_pair(acts_in, w_one, p), 0.0)
        put_shifted(acts_mid, 2 * p, value[:, :BX], first, last)
        put_shifted(acts_mid, 2 * p + 1, value[:, BX:], first, last)

    def conv_two(p):
        base = (2 * p + 1) * TAPS + ROWS
        own = jnp.concatenate(
            [acts_in[base : base + ROWS, :], acts_in[base + TAPS : base + TAPS + ROWS, :]], axis=1
        )
        value = conv_pair(acts_mid, w_two, p) + own.astype(f32)
        return jnp.maximum(value, 0.0).astype(bf16)

    def head(s, p, acts):
        value = jnp.dot(w_top[...], acts, preferred_element_type=f32)
        pair = [value[:, :BX] * BLEND[2 * p], value[:, BX:] * BLEND[2 * p + 1]]
        if p == 0:
            low[s] = jnp.concatenate(pair, axis=0).astype(bf16)
        elif p == 5:
            high[s] = jnp.concatenate(pair, axis=0).astype(bf16)
        else:
            result[s, 2 * p - 2] = pair[0]
            result[s, 2 * p - 1] = pair[1]

    def close(s):
        for copy in edges(s):
            copy.wait()
        finish(result, from_lower, from_upper, finished, s, level)

    for copy in halos(0):
        copy.wait()
    prepare(0, 0)
    prepare(0, 1)

    @pl.loop(0, slots)
    def _(s):
        before(s)
        previous = jnp.maximum(s - 1, 0)
        conv_one(0)
        prepare(s, 2)
        acts_4 = conv_two(4)
        conv_one(1)
        prepare(s, 3)
        head(previous, 4, acts_4)
        acts_5 = conv_two(5)
        conv_one(2)
        prepare(s, 4)
        head(previous, 5, acts_5)
        acts_0 = conv_two(0)
        conv_one(3)
        prepare(s, 5)
        acts_1 = conv_two(1)
        head(s, 0, acts_0)
        conv_one(4)
        acts_2 = conv_two(2)
        head(s, 1, acts_1)
        conv_one(5)

        @pl.when(s > 0)
        def _():
            for copy in edges(s - 1):
                copy.start()

        @pl.when(s < slots - 1)
        def _():
            for copy in halos(s + 1):
                copy.wait()

        following = jnp.minimum(s + 1, slots - 1)
        acts_3 = conv_two(3)
        head(s, 2, acts_2)
        prepare(following, 0)
        prepare(following, 1)
        head(s, 3, acts_3)

        @pl.when(s > 1)
        def _():
            close(s - 2)

    acts_4 = conv_two(4)
    acts_5 = conv_two(5)
    head(slots - 1, 4, acts_4)
    head(slots - 1, 5, acts_5)
    for copy in edges(slots - 1):
        copy.start()
    close(slots - 2)
    close(slots - 1)


def build_banded(taps, mixed, banded):
    blocks = []
    for outer in range(9):
        rows = [((outer // 3 * 3 + dy) * 3 + outer % 3) * C for dy in range(3)]
        blocks.append(
            jnp.concatenate([taps[at : at + C, :].astype(f32) for at in rows], axis=1)
        )
    stacked = jnp.concatenate(blocks, axis=0).astype(bf16)
    row, col = iota((3 * C, ROWS), 0), iota((3 * C, ROWS), 1)
    same = row % C == col // BY
    for y in range(BY):
        spread = (same & (col % BY == y + row // C - 1)).astype(bf16)
        wide = jnp.dot(stacked, spread, preferred_element_type=f32).astype(bf16)
        for outer in range(9):
            mixed[y * C : (y + 1) * C, outer * ROWS : (outer + 1) * ROWS] = wide[
                outer * C : (outer + 1) * C
            ]
    row, col = iota((ROWS, ROWS), 0), iota((ROWS, ROWS), 1)
    order = ((row // BY == col % C) & (row % BY == col // C)).astype(bf16)
    for outer in range(9):
        cut = slice(outer * ROWS, (outer + 1) * ROWS)
        banded[:, cut] = jnp.dot(order, mixed[:, cut], preferred_element_type=f32).astype(bf16)


def build_head(w_head, banded):
    spread = (iota((C, ROWS), 1) // BY == iota((C, ROWS), 0)).astype(bf16)
    wide = jnp.dot(w_head[...], spread, preferred_element_type=f32)
    wide = jnp.broadcast_to(wide[:, None, :], (AFF, BY, ROWS)).reshape(AFF * BY, ROWS)
    apart = iota((AFF * BY, ROWS), 1) % BY - iota((AFF * BY, ROWS), 0) % BY
    banded[...] = jnp.where(apart == 0, wide, 0.0).astype(bf16)


DEPTH = 4


def running_counts(occupied):
    running = []
    count = jnp.int32(0)
    for b in range(BLK):
        count = count + occupied[b]
        running.append(count)
    return running


def block_of_rank(running, rank):
    picked = jnp.int32(0)
    for b in range(BLK):
        picked = picked + jnp.where(running[b] <= rank, 1, 0)
    return jnp.minimum(picked, BLK - 1)


def halo_copies(tiles, send, recv, above, below, s):
    down = pltpu.make_async_remote_copy(
        src_ref=tiles.at[s, :, 16:32, :],
        dst_ref=tiles.at[s, :, 80:96, :],
        send_sem=send.at[s, 0],
        recv_sem=recv.at[s, 0],
        device_id=below,
        device_id_type=MESH,
    )
    up = pltpu.make_async_remote_copy(
        src_ref=tiles.at[s, :, 64:80, :],
        dst_ref=tiles.at[s, :, 0:16, :],
        send_sem=send.at[s, 1],
        recv_sem=recv.at[s, 1],
        device_id=above,
        device_id_type=MESH,
    )
    return down, up


def edge_copies(low, high, from_upper, from_lower, send, recv, above, below, s):
    down = pltpu.make_async_remote_copy(
        src_ref=low.at[s],
        dst_ref=from_upper.at[s],
        send_sem=send.at[s, 0],
        recv_sem=recv.at[s, 0],
        device_id=below,
        device_id_type=MESH,
    )
    up = pltpu.make_async_remote_copy(
        src_ref=high.at[s],
        dst_ref=from_lower.at[s],
        send_sem=send.at[s, 1],
        recv_sem=recv.at[s, 1],
        device_id=above,
        device_id_type=MESH,
    )
    return down, up


def finish(result, from_lower, from_upper, finished, s, level):
    has_lower, has_upper = level > 0, level < DEPTH - 1
    planes = [result[s, z] for z in range(ZD)]
    lower = from_lower[s].astype(f32)
    upper = from_upper[s].astype(f32)
    for i in range(2):
        part = lower[24 * i : 24 * i + 24]
        planes[i] = jnp.where(has_lower, planes[i] + part, planes[i] / BLEND[2 + i])
        part = upper[24 * i : 24 * i + 24]
        planes[6 + i] = jnp.where(has_upper, planes[6 + i] + part, planes[6 + i] / BLEND[8 + i])
    for a in range(AFF):
        for p in range(4):
            two = [planes[2 * p + i][BY * a : BY * a + BY] for i in range(2)]
            finished[s, a, 16 * p : 16 * p + 16, :] = jnp.concatenate(two, axis=0).astype(bf16)


def whole_kernel(
    slots,
    occupied,
    features,
    taps_one,
    taps_two,
    w_head,
    out,
    held,
    tiles,
    acts_in,
    acts_mid,
    w_one,
    w_two,
    w_top,
    mixed,
    result,
    low,
    high,
    from_upper,
    from_lower,
    finished,
    load_sem,
    halo_send,
    halo_recv,
    edge_send,
    edge_recv,
):
    wide = lax.axis_index("wide")
    level = lax.axis_index("narrow")
    above = (wide, lax.rem(level + 1, DEPTH))
    below = (wide, lax.rem(level + DEPTH - 1, DEPTH))

    load = pltpu.make_async_copy(features, held, load_sem)
    load.start()
    barrier = pltpu.get_barrier_semaphore()
    for neighbour in (above, below):
        pl.semaphore_signal(barrier, inc=1, device_id=neighbour, device_id_type=MESH)
    pl.semaphore_wait(barrier, 2)

    running = running_counts(occupied)
    halos = functools.partial(halo_copies, tiles, halo_send, halo_recv, above, below)
    edges = functools.partial(
        edge_copies, low, high, from_upper, from_lower, edge_send, edge_recv, above, below
    )
    load.wait()

    @pl.loop(0, slots)
    def _(s):
        tiles[s, :, 16:80, :] = held[block_of_rank(running, s)]
        for copy in halos(s):
            copy.start()

    for planes in (acts_in, acts_mid):
        planes[0:TAPS, :] = jnp.zeros((TAPS, BX), bf16)
        planes[(TZ + 1) * TAPS : (TZ + 2) * TAPS, :] = jnp.zeros((TAPS, BX), bf16)
    build_banded(taps_one, mixed, w_one)
    build_banded(taps_two, mixed, w_two)
    build_head(w_head, w_top)

    work_through(
        slots,
        level,
        tiles,
        acts_in,
        acts_mid,
        w_one,
        w_two,
        w_top,
        result,
        low,
        high,
        finished,
        from_lower,
        from_upper,
        halos,
        edges,
        lambda s: None,
    )

    for b in range(BLK):
        kept = finished[running[b] - occupied[b]]
        out[b] = jnp.where(occupied[b] > 0, kept, jnp.zeros_like(kept))


SLOTS = 7
SURE = 3
GROUPS = ((0, 4, 3), (4, 8, 4), (8, 10, 5))
LANES = 10
TWINS = 4
TARGET = 5
COLUMNS = 32


def lane_step(lane, core):
    if lane < 8:
        sign = (1, -1, 1, -1)[lane - TWINS]
        return (sign, 0) if lane < TWINS + 2 else (0, sign)
    sign = (1, -1)[lane - 8]
    return sign * (1 - core), sign * core


def column_at(x, y, core):
    return (x % 4 * 4 + y % 4) * 2 + core


def lane_columns(lane, sign):
    column = lax.axis_index("wide")
    core, y, x = column % 2, column // 2 % 4, column // 8
    if lane < TWINS:
        return column_at(x, y, 1 - core)
    over_x, over_y = lane_step(lane, core)
    return column_at(x + sign * over_x + 4, y + sign * over_y + 4, core)


def turned(value, dim, step):
    step = step % 4
    if step == 0:
        return value
    head = lax.slice_in_dim(value, 0, step, axis=dim)
    return jnp.concatenate([lax.slice_in_dim(value, step, 4, axis=dim), head], axis=dim)


def across(value, kind, sign):
    if kind == 0:
        return jnp.concatenate([value[:, :, 1:2], value[:, :, 0:1]], axis=2)
    if kind < 5:
        over_x, over_y = lane_step(kind + TWINS - 1, 0)
        return turned(turned(value, 0, sign * over_x), 1, sign * over_y)
    step = sign * (1, -1)[kind - 5]
    over_x, over_y = turned(value, 0, step), turned(value, 1, step)
    return jnp.concatenate([over_x[:, :, 0:1], over_y[:, :, 1:2]], axis=2)


def make_plan(counts, used):
    load = counts
    own = counts
    kinds = 7
    for turn in range(2):
        for kind in range(kinds):
            gap = load - across(load, kind, 1)
            before = used[kind].reshape(load.shape) if turn > 0 else jnp.zeros_like(load)
            if kind == 0:
                sends = jnp.minimum(jnp.minimum(TWINS - before, own), gap >> 1)
                sends = jnp.maximum(jnp.minimum(sends, load - TARGET), 0)
            else:
                sends = (load > TARGET) & (gap >= 2) & (own > 0) & (before == 0)
                sends = jnp.where(sends, 1, 0)
            used[kind] = (before + sends).reshape(used.shape[1:])
            own = own - sends
            load = load - sends + across(sends, kind, -1)
    need = jnp.maximum(own, SURE)
    for kinds, start in (((0,), 3), ((1, 2, 3, 4), 4), ((5, 6), 5)):
        taken = jnp.zeros_like(load)
        for kind in kinds:
            taken = taken + across(used[kind].reshape(load.shape), kind, -1)
        need = jnp.where(taken > 0, jnp.maximum(need, start) + taken, need)
    used[7, 0] = jnp.max(need.reshape((COLUMNS,) + need.shape[3:]), axis=0)


def shared_kernel(
    occupied,
    features,
    taps_one,
    taps_two,
    w_head,
    out,
    needed,
    held,
    tiles,
    acts_in,
    acts_mid,
    w_one,
    w_two,
    w_top,
    mixed,
    result,
    low,
    high,
    from_upper,
    from_lower,
    finished,
    counts,
    used,
    out_a,
    out_b,
    out_c,
    in_a,
    in_b,
    in_c,
    back_out,
    back_in,
    load_sem,
    count_send,
    count_recv,
    lane_send,
    lane_recv,
    back_send,
    back_recv,
    halo_send,
    halo_recv,
    edge_send,
    edge_recv,
):
    wide = lax.axis_index("wide")
    level = lax.axis_index("narrow")
    above = (wide, lax.rem(level + 1, DEPTH))
    below = (wide, lax.rem(level + DEPTH - 1, DEPTH))

    core, y, x = wide % 2, wide // 2 % 4, wide // 8

    load = pltpu.make_async_copy(features, held, load_sem)
    load.start()
    peers = [
        [column_at(x, y, 1 - core)],
        [column_at(x, y + d, core) for d in (1, 2, 3)],
        [column_at(x + d, y, core) for d in (1, 2, 3)],
    ]
    barrier = pltpu.get_barrier_semaphore()
    greeted = [above, below] + [(column, level) for part in peers for column in part]
    for device in greeted:
        pl.semaphore_signal(barrier, inc=1, device_id=device, device_id_type=MESH)

    running = running_counts(occupied)
    held_blocks = running[-1]
    counts[x, y, core] = jnp.full((8, 128), held_blocks, jnp.int32)
    parts = [counts.at[x, y, core], counts.at[x, y], counts.at[x]]

    def count_copies(turn):
        copies = []
        for d, column in enumerate(peers[turn]):
            at = 3 * turn + d
            copies.append(
                pltpu.make_async_remote_copy(
                    src_ref=parts[turn],
                    dst_ref=parts[turn],
                    send_sem=count_send.at[at],
                    recv_sem=count_recv.at[at],
                    device_id=(column, level),
                    device_id_type=MESH,
                )
            )
        return copies

    outs, ins = (out_a, out_b, out_c), (in_a, in_b, in_c)

    def lane_copy(group, lane):
        at = lane - GROUPS[group][0]
        return pltpu.make_async_remote_copy(
            src_ref=outs[group].at[at],
            dst_ref=ins[group].at[at],
            send_sem=lane_send.at[lane],
            recv_sem=lane_recv.at[lane],
            device_id=(lane_columns(lane, 1), level),
            device_id_type=MESH,
        )

    def back_copy(lane):
        return pltpu.make_async_remote_copy(
            src_ref=back_out.at[lane],
            dst_ref=back_in.at[lane],
            send_sem=back_send.at[lane],
            recv_sem=back_recv.at[lane],
            device_id=(lane_columns(lane, -1), level),
            device_id_type=MESH,
        )

    halos = functools.partial(halo_copies, tiles, halo_send, halo_recv, above, below)
    edges = functools.partial(
        edge_copies, low, high, from_upper, from_lower, edge_send, edge_recv, above, below
    )

    build_banded(taps_one, mixed, w_one)
    for planes in (acts_in, acts_mid):
        planes[0:TAPS, :] = jnp.zeros((TAPS, BX), bf16)
        planes[(TZ + 1) * TAPS : (TZ + 2) * TAPS, :] = jnp.zeros((TAPS, BX), bf16)
    pl.semaphore_wait(barrier, len(greeted))
    for copy in count_copies(0):
        copy.start()
    load.wait()
    for s in range(SURE):
        tiles[s, :, 16:80, :] = held[block_of_rank(running, s)]
        for copy in halos(s):
            copy.start()
    for copy in count_copies(0):
        copy.wait()
    for copy in count_copies(1):
        copy.start()
    build_banded(taps_two, mixed, w_two)
    for copy in count_copies(1):
        copy.wait()
    for copy in count_copies(2):
        copy.start()
    build_head(w_head, w_top)
    for copy in count_copies(2):
        copy.wait()

    make_plan(counts[...], used)
    needed[0] = used[7, 0, 0, 0]
    sent, taken = [], []
    for lane in range(LANES):
        source = lane_columns(lane, -1)
        if lane < TWINS:
            sent.append(jnp.where(used[0, wide, 0, 0] > lane, 1, 0))
            taken.append(jnp.where(used[0, source, 0, 0] > lane, 1, 0))
        else:
            sent.append(used[lane - TWINS + 1, wide, 0, 0])
            taken.append(used[lane - TWINS + 1, source, 0, 0])
    kept = held_blocks - sum(sent)
    ranks = []
    rank = kept
    for lane in range(LANES):
        ranks.append(rank)
        rank = rank + sent[lane]
    places = []
    place = jnp.maximum(kept, SURE)
    for start, end, first in GROUPS:
        place = jnp.maximum(place, first)
        for lane in range(start, end):
            places.append(place)
            place = place + taken[lane]

    def send(group):
        start, end, _ = GROUPS[group]
        for lane in range(start, end):
            outs[group][lane - start] = held[block_of_rank(running, ranks[lane])]
            lane_copy(group, lane).start()

    def receive(group):
        for lane in range(*GROUPS[group][:2]):
            lane_copy(group, lane).wait()

    def stage(s):
        value = held[block_of_rank(running, s)]
        for group, (start, end, first) in enumerate(GROUPS):
            if s < first:
                continue
            chosen, found = jnp.int32(0), jnp.int32(0)
            for lane in range(start, end):
                here = (taken[lane] > 0) & (places[lane] == s)
                chosen = chosen + jnp.where(here, lane - start, 0)
                found = found + jnp.where(here, 1, 0)
            value = jnp.where(found > 0, ins[group][chosen], value)
        tiles[s, :, 16:80, :] = value
        for copy in halos(s):
            copy.start()

    send(0)
    send(1)

    def before(s):
        @pl.when(s == 2)
        def _():
            receive(0)
            stage(3)
            send(2)

        @pl.when(s == 3)
        def _():
            receive(1)
            stage(4)

        @pl.when(s == 4)
        def _():
            receive(2)
            stage(5)
            stage(6)

    work_through(
        SLOTS,
        level,
        tiles,
        acts_in,
        acts_mid,
        w_one,
        w_two,
        w_top,
        result,
        low,
        high,
        finished,
        from_lower,
        from_upper,
        halos,
        edges,
        before,
    )

    for lane in range(LANES):
        back_out[lane] = finished[jnp.clip(places[lane], 0, SLOTS - 1)]
        back_copy(lane).start()
    for lane in range(LANES):
        back_copy(lane).wait()

    for b in range(BLK):
        rank = running[b] - occupied[b]
        chosen = jnp.int32(0)
        for lane in range(LANES):
            chosen = chosen + jnp.where((sent[lane] > 0) & (ranks[lane] == rank), lane, 0)
        local = finished[jnp.minimum(rank, SLOTS - 1)]
        value = jnp.where(rank < kept, local, back_in[chosen])
        out[b] = jnp.where(occupied[b] > 0, value, jnp.zeros_like(value))


def work_scratch(slots):
    return [
        pltpu.VMEM((BLK, C, ZD * BY, BX), bf16),
        pltpu.VMEM((slots, C, TZ * BY, BX), bf16),
        pltpu.VMEM(((TZ + 2) * TAPS, BX), bf16),
        pltpu.VMEM(((TZ + 2) * TAPS, BX), bf16),
        pltpu.VMEM((ROWS, 9 * ROWS), bf16),
        pltpu.VMEM((ROWS, 9 * ROWS), bf16),
        pltpu.VMEM((AFF * BY, ROWS), bf16),
        pltpu.VMEM((ROWS, 9 * ROWS), bf16),
        pltpu.VMEM((slots, ZD, AFF * BY, BX), f32),
        pltpu.VMEM((slots, 2 * AFF * BY, BX), bf16),
        pltpu.VMEM((slots, 2 * AFF * BY, BX), bf16),
        pltpu.VMEM((slots, 2 * AFF * BY, BX), bf16),
        pltpu.VMEM((slots, 2 * AFF * BY, BX), bf16),
        pltpu.VMEM((slots, AFF, ZD * BY, BX), bf16),
    ]


def on_device(features, occupied, w_first, w_second, w_head):
    vmem = pl.BlockSpec(memory_space=pltpu.VMEM)
    in_specs = [
        pl.BlockSpec(memory_space=pltpu.SMEM),
        pl.BlockSpec(memory_space=pl.ANY),
        vmem,
        vmem,
        vmem,
    ]
    affinities = jax.ShapeDtypeStruct((BLK, AFF, ZD * BY, BX), bf16)
    dma = pltpu.SemaphoreType.DMA
    shared = pl.pallas_call(
        shared_kernel,
        out_shape=[affinities, jax.ShapeDtypeStruct((1,), jnp.int32)],
        in_specs=in_specs,
        out_specs=[vmem, pl.BlockSpec(memory_space=pltpu.SMEM)],
        scratch_shapes=work_scratch(SLOTS)
        + [
            pltpu.VMEM((4, 4, 2, 8, 128), jnp.int32),
            pltpu.VMEM((8, COLUMNS, 8, 128), jnp.int32),
        ]
        + [pltpu.VMEM((end - start, C, ZD * BY, BX), bf16) for start, end, _ in GROUPS * 2]
        + [
            pltpu.VMEM((LANES, AFF, ZD * BY, BX), bf16),
            pltpu.VMEM((LANES, AFF, ZD * BY, BX), bf16),
            dma,
            dma((9,)),
            dma((9,)),
            dma((LANES,)),
            dma((LANES,)),
            dma((LANES,)),
            dma((LANES,)),
            dma((SLOTS, 2)),
            dma((SLOTS, 2)),
            dma((SLOTS, 2)),
            dma((SLOTS, 2)),
        ],
        compiler_params=pltpu.CompilerParams(
            collective_id=0, has_side_effects=True, vmem_limit_bytes=56 << 20
        ),
    )
    whole = pl.pallas_call(
        functools.partial(whole_kernel, BLK),
        out_shape=affinities,
        in_specs=in_specs,
        out_specs=vmem,
        scratch_shapes=work_scratch(BLK)
        + [dma, dma((BLK, 2)), dma((BLK, 2)), dma((BLK, 2)), dma((BLK, 2))],
        compiler_params=pltpu.CompilerParams(
            collective_id=1, has_side_effects=True, vmem_limit_bytes=56 << 20
        ),
    )
    taps = [
        jnp.transpose(w, (2, 3, 4, 0, 1)).reshape(27 * C, C) for w in (w_first, w_second)
    ]
    args = (occupied, features.reshape(BLK, C, ZD * BY, BX), *taps, w_head)
    out, needed = shared(*args)
    out = lax.cond(needed[0] > SLOTS, lambda: whole(*args), lambda: out)
    return out.reshape(BLK, AFF, ZD, BY, BX)


def solution(mesh):
    in_specs = (P("wide", None, "narrow", None, None), P("wide"), P(), P(), P())
    out_specs = P("wide", None, "narrow", None, None)
    return jax.shard_map(
        on_device, mesh=mesh, in_specs=in_specs, out_specs=out_specs, check_vma=False
    )
```

time: 69.7 us -> 68.1 us (0.977); the launches traced: 68.6 us -> 68 us
  local copies, waits for them, and re-layouts: 2.09 us -> 0.9 us
    slice x1 -> x0, local copies, waits for them, and re-layouts: 1.19 us -> none  [on_device(): out = lax.cond(needed[0, 0] > SLOTS, lambda: whole(*args), lambda: out)]
where the time goes in v3:
time: 68.1 us; the launch traced here: 68 us
  Pallas kernels  66.2 us (97%)
  local copies, waits for them, and re-layouts  0.9 us (1%)
  between operations  0.74 us (1%)
    pallas_call x1, Pallas kernels, on_device(): out, needed = shared(*args)  66.2 us

profile of v3, /device:TPU:0, one launch (start us, length us, event | category | flops | bytes accessed | tf_op | source)
XLA Modules:
  0.0 68.0 jit_solution(15253061053688128621)
XLA Ops:
  0.0 0.0 copy-start.2
  0.0 0.0 copy-start.3
  0.0 0.0 copy-start.1
  0.0 0.0 copy-start
  0.0 66.2 %shard_map.57 = (bf16[16,3,64,128]{3,2,1,0:T(8,128)(2,1)S(1)}, s32[1]{0:T(128)}) custom-call(s32[16]{0:T(128)} %occupied.1, bf16[16,32,64,128]{3,2,1,0:T(8,128)(2,1)} %bitcast.10, bf16[864,32]{1,0:T(8,128)(2,1)} %bitcast.12, bf16[864,32]{1,0:T(8,128)(2,1)} %bitcast.14, bf16[3,32]{1,0:T(4,128)(2,1)} %w_head.1), custom_call_target="tpu_custom_call" | custom-call | tf_op jit(solution)/shard_map/pallas_call | solution.py:755
  66.9 0.0 copy-done.2
  66.9 0.0 copy-done.3
  66.9 0.0 copy-done.1
  66.9 0.0 copy-done
  66.9 0.2 conditional.1
  67.1 0.9 %copy.12 = bf16[16,3,8,8,128]{4,3,2,1,0:T(8,128)(2,1)} copy(bf16[16,3,8,8,128]{4,3,2,1,0:T(8,128)(2,1)S(1)} %get-tuple-element.30) | data formatting | bytes 1572864
Async XLA Ops:
  0.0 66.9 %copy-start.2 = (bf16[3,32]{1,0:T(4,128)(2,1)S(1)}, bf16[3,32]{1,0:T(4,128)(2,1)}, u32[]{:S(2)}) copy-start(bf16[3,32]{1,0:T(4,128)(2,1)} %w_head.1) | copy-start | bytes 580
  0.0 66.9 %copy-start.3 = (s32[16]{0:T(128)S(1)}, s32[16]{0:T(128)}, u32[]{:S(2)}) copy-start(s32[16]{0:T(128)} %occupied.1) | copy-start | bytes 196
  0.0 66.9 %copy-start.1 = (bf16[32,32,3,3,3]{1,0,4,3,2:T(8,128)(2,1)S(1)}, bf16[32,32,3,3,3]{1,0,4,3,2:T(8,128)(2,1)}, u32[]{:S(2)}) copy-start(bf16[32,32,3,3,3]{1,0,4,3,2:T(8,128)(2,1)} %param.10) | copy-start | bytes 165892
  0.0 66.9 %copy-start = (bf16[32,32,3,3,3]{1,0,4,3,2:T(8,128)(2,1)S(1)}, bf16[32,32,3,3,3]{1,0,4,3,2:T(8,128)(2,1)}, u32[]{:S(2)}) copy-start(bf16[32,32,3,3,3]{1,0,4,3,2:T(8,128)(2,1)} %param.9) | copy-start | bytes 165892

commit v4 on v3

--- a/solution.py
+++ b/solution.py
@@ -106,25 +106,34 @@
             copy.wait()
         finish(result, from_lower, from_upper, finished, s, level)
 
-    for copy in halos(0):
-        copy.wait()
-    prepare(0, 0)
-    prepare(0, 1)
-
     @pl.loop(0, slots)
     def _(s):
         before(s)
+
+        @pl.when(s > 1)
+        def _():
+            for copy in edges(s - 2):
+                copy.start()
+
+        @pl.when(s > 2)
+        def _():
+            close(s - 3)
+
+        for copy in halos(s):
+            copy.wait()
         previous = jnp.maximum(s - 1, 0)
+        acts_4 = conv_two(4)
+        prepare(s, 0)
+        prepare(s, 1)
+        acts_5 = conv_two(5)
         conv_one(0)
         prepare(s, 2)
-        acts_4 = conv_two(4)
+        head(previous, 4, acts_4)
         conv_one(1)
         prepare(s, 3)
-        head(previous, 4, acts_4)
-        acts_5 = conv_two(5)
+        head(previous, 5, acts_5)
         conv_one(2)
         prepare(s, 4)
-        head(previous, 5, acts_5)
         acts_0 = conv_two(0)
         conv_one(3)
         prepare(s, 5)
@@ -134,36 +143,20 @@
         acts_2 = conv_two(2)
         head(s, 1, acts_1)
         conv_one(5)
-
-        @pl.when(s > 0)
-        def _():
-            for copy in edges(s - 1):
-                copy.start()
-
-        @pl.when(s < slots - 1)
-        def _():
-            for copy in halos(s + 1):
-                copy.wait()
-
-        following = jnp.minimum(s + 1, slots - 1)
         acts_3 = conv_two(3)
         head(s, 2, acts_2)
-        prepare(following, 0)
-        prepare(following, 1)
         head(s, 3, acts_3)
 
-        @pl.when(s > 1)
-        def _():
-            close(s - 2)
-
+    for copy in edges(slots - 2):
+        copy.start()
     acts_4 = conv_two(4)
     acts_5 = conv_two(5)
     head(slots - 1, 4, acts_4)
     head(slots - 1, 5, acts_5)
     for copy in edges(slots - 1):
         copy.start()
-    close(slots - 2)
-    close(slots - 1)
+    for s in range(slots - 3, slots):
+        close(s)
 
 
 def build_banded(taps, mixed, banded):
@@ -545,18 +538,10 @@
         edge_copies, low, high, from_upper, from_lower, edge_send, edge_recv, above, below
     )
 
-    build_banded(taps_one, mixed, w_one)
-    for planes in (acts_in, acts_mid):
-        planes[0:TAPS, :] = jnp.zeros((TAPS, BX), bf16)
-        planes[(TZ + 1) * TAPS : (TZ + 2) * TAPS, :] = jnp.zeros((TAPS, BX), bf16)
     pl.semaphore_wait(barrier, len(greeted))
     for copy in count_copies(0):
         copy.start()
-    load.wait()
-    for s in range(SURE):
-        tiles[s, :, 16:80, :] = held[block_of_rank(running, s)]
-        for copy in halos(s):
-            copy.start()
+    build_banded(taps_one, mixed, w_one)
     for copy in count_copies(0):
         copy.wait()
     for copy in count_copies(1):
@@ -566,36 +551,50 @@
         copy.wait()
     for copy in count_copies(2):
         copy.start()
+    load.wait()
+
+    def stage_own(s):
+        tiles[s, :, 16:80, :] = held[block_of_rank(running, s)]
+        for copy in halos(s):
+            copy.start()
+
+    stage_own(0)
     build_head(w_head, w_top)
+    for planes in (acts_in, acts_mid):
+        planes[0:TAPS, :] = jnp.zeros((TAPS, BX), bf16)
+        planes[(TZ + 1) * TAPS : (TZ + 2) * TAPS, :] = jnp.zeros((TAPS, BX), bf16)
     for copy in count_copies(2):
         copy.wait()
-
     make_plan(counts[...], used)
     needed[0] = used[7, 0, 0, 0]
-    sent, taken = [], []
-    for lane in range(LANES):
-        source = lane_columns(lane, -1)
-        if lane < TWINS:
-            sent.append(jnp.where(used[0, wide, 0, 0] > lane, 1, 0))
-            taken.append(jnp.where(used[0, source, 0, 0] > lane, 1, 0))
-        else:
-            sent.append(used[lane - TWINS + 1, wide, 0, 0])
-            taken.append(used[lane - TWINS + 1, source, 0, 0])
-    kept = held_blocks - sum(sent)
-    ranks = []
-    rank = kept
-    for lane in range(LANES):
-        ranks.append(rank)
-        rank = rank + sent[lane]
-    places = []
-    place = jnp.maximum(kept, SURE)
-    for start, end, first in GROUPS:
-        place = jnp.maximum(place, first)
-        for lane in range(start, end):
-            places.append(place)
-            place = place + taken[lane]
+
+    def schedule():
+        sent, taken = [], []
+        for lane in range(LANES):
+            source = lane_columns(lane, -1)
+            if lane < TWINS:
+                sent.append(jnp.where(used[0, wide, 0, 0] > lane, 1, 0))
+                taken.append(jnp.where(used[0, source, 0, 0] > lane, 1, 0))
+            else:
+                sent.append(used[lane - TWINS + 1, wide, 0, 0])
+                taken.append(used[lane - TWINS + 1, source, 0, 0])
+        kept = held_blocks - sum(sent)
+        ranks = []
+        rank = kept
+        for lane in range(LANES):
+            ranks.append(rank)
+            rank = rank + sent[lane]
+        places = []
+        place = jnp.maximum(kept, SURE)
+        for start, end, first in GROUPS:
+            place = jnp.maximum(place, first)
+            for lane in range(start, end):
+                places.append(place)
+                place = place + taken[lane]
+        return kept, sent, ranks, taken, places
 
     def send(group):
+        ranks = schedule()[2]
         start, end, _ = GROUPS[group]
         for lane in range(start, end):
             outs[group][lane - start] = held[block_of_rank(running, ranks[lane])]
@@ -606,6 +605,7 @@
             lane_copy(group, lane).wait()
 
     def stage(s):
+        _, _, _, taken, places = schedule()
         value = held[block_of_rank(running, s)]
         for group, (start, end, first) in enumerate(GROUPS):
             if s < first:
@@ -620,10 +620,11 @@
         for copy in halos(s):
             copy.start()
 
-    send(0)
-    send(1)
-
     def before(s):
+        @pl.when(s < SURE - 1)
+        def _():
+            stage_own(s + 1)
+
         @pl.when(s == 2)
         def _():
             receive(0)
@@ -639,8 +640,13 @@
         def _():
             receive(2)
             stage(5)
+
+        @pl.when(s == 5)
+        def _():
             stage(6)
 
+    send(1)
+    send(0)
     work_through(
         SLOTS,
         level,
@@ -661,7 +667,8 @@
         before,
     )
 
-    for lane in range(LANES):
+    kept, sent, ranks, _, places = schedule()
+    for lane in reversed(range(LANES)):
         back_out[lane] = finished[jnp.clip(places[lane], 0, SLOTS - 1)]
         back_copy(lane).start()
     for lane in range(LANES):

time: 68.1 us -> 63.5 us (0.932)
  Pallas kernels: 66.2 us -> 61.5 us
    pallas_call x1, Pallas kernels: 66.2 us -> 61.5 us  [on_device(): out, needed = shared(*args)]
where the time goes in v4:
time: 63.5 us; the launch traced here: 63.4 us
  Pallas kernels  61.5 us (97%)
  local copies, waits for them, and re-layouts  0.9 us (1%)
  between operations  0.74 us (1%)
    pallas_call x1, Pallas kernels, on_device(): out, needed = shared(*args)  61.5 us

profile of v4, /device:TPU:0, one launch (start us, length us, event | category | flops | bytes accessed | tf_op | source)
XLA Modules:
  0.0 63.4 jit_solution(4044877460377392367)
XLA Ops:
  0.0 0.0 copy-start.2
  0.0 0.0 copy-start.3
  0.0 0.0 copy-start.1
  0.0 0.0 copy-start
  0.0 61.5 %shard_map.57 = (bf16[16,3,64,128]{3,2,1,0:T(8,128)(2,1)S(1)}, s32[1]{0:T(128)}) custom-call(s32[16]{0:T(128)} %occupied.1, bf16[16,32,64,128]{3,2,1,0:T(8,128)(2,1)} %bitcast.10, bf16[864,32]{1,0:T(8,128)(2,1)} %bitcast.12, bf16[864,32]{1,0:T(8,128)(2,1)} %bitcast.14, bf16[3,32]{1,0:T(4,128)(2,1)} %w_head.1), custom_call_target="tpu_custom_call" | custom-call | tf_op jit(solution)/shard_map/pallas_call | solution.py:762
  62.2 0.0 copy-done.2
  62.2 0.0 copy-done.3
  62.3 0.0 copy-done.1
  62.3 0.0 copy-done
  62.3 0.2 conditional.1
  62.5 0.9 %copy.12 = bf16[16,3,8,8,128]{4,3,2,1,0:T(8,128)(2,1)} copy(bf16[16,3,8,8,128]{4,3,2,1,0:T(8,128)(2,1)S(1)} %get-tuple-element.30) | data formatting | bytes 1572864
Async XLA Ops:
  0.0 62.2 %copy-start.2 = (bf16[3,32]{1,0:T(4,128)(2,1)S(1)}, bf16[3,32]{1,0:T(4,128)(2,1)}, u32[]{:S(2)}) copy-start(bf16[3,32]{1,0:T(4,128)(2,1)} %w_head.1) | copy-start | bytes 580
  0.0 62.2 %copy-start.3 = (s32[16]{0:T(128)S(1)}, s32[16]{0:T(128)}, u32[]{:S(2)}) copy-start(s32[16]{0:T(128)} %occupied.1) | copy-start | bytes 196
  0.0 62.3 %copy-start.1 = (bf16[32,32,3,3,3]{1,0,4,3,2:T(8,128)(2,1)S(1)}, bf16[32,32,3,3,3]{1,0,4,3,2:T(8,128)(2,1)}, u32[]{:S(2)}) copy-start(bf16[32,32,3,3,3]{1,0,4,3,2:T(8,128)(2,1)} %param.10) | copy-start | bytes 165892
  0.0 62.3 %copy-start = (bf16[32,32,3,3,3]{1,0,4,3,2:T(8,128)(2,1)S(1)}, bf16[32,32,3,3,3]{1,0,4,3,2:T(8,128)(2,1)}, u32[]{:S(2)}) copy-start(bf16[32,32,3,3,3]{1,0,4,3,2:T(8,128)(2,1)} %param.9) | copy-start | bytes 165892

commit v5 on v4

--- a/solution.py
+++ b/solution.py
@@ -356,7 +356,7 @@
 GROUPS = ((0, 4, 3), (4, 8, 4), (8, 10, 5))
 LANES = 10
 TWINS = 4
-TARGET = 5
+TARGETS = (6, 5)
 COLUMNS = 32
 
 
@@ -403,16 +403,15 @@
 def make_plan(counts, used):
     load = counts
     own = counts
-    kinds = 7
-    for turn in range(2):
-        for kind in range(kinds):
+    for turn, target in enumerate(TARGETS):
+        for kind in (0, 5, 6, 1, 2, 3, 4):
             gap = load - across(load, kind, 1)
             before = used[kind].reshape(load.shape) if turn > 0 else jnp.zeros_like(load)
             if kind == 0:
                 sends = jnp.minimum(jnp.minimum(TWINS - before, own), gap >> 1)
-                sends = jnp.maximum(jnp.minimum(sends, load - TARGET), 0)
+                sends = jnp.maximum(jnp.minimum(sends, load - target), 0)
             else:
-                sends = (load > TARGET) & (gap >= 2) & (own > 0) & (before == 0)
+                sends = (load > target) & (gap >= 2) & (own > 0) & (before == 0)
                 sends = jnp.where(sends, 1, 0)
             used[kind] = (before + sends).reshape(used.shape[1:])
             own = own - sends

time: 63.5 us -> 63.5 us (level)
  no operation moved by 1% of the time
where the time goes in v5:
time: 63.5 us; the launch traced here: 63.4 us
  Pallas kernels  61.5 us (97%)
  local copies, waits for them, and re-layouts  0.9 us (1%)
  between operations  0.74 us (1%)
    pallas_call x1, Pallas kernels, on_device(): out, needed = shared(*args)  61.5 us

profile of v5, /device:TPU:0, one launch (start us, length us, event | category | flops | bytes accessed | tf_op | source)
XLA Modules:
  0.0 63.4 jit_solution(12343352916494353323)
XLA Ops:
  0.0 0.0 copy-start.2
  0.0 0.0 copy-start.3
  0.0 0.0 copy-start.1
  0.0 0.0 copy-start
  0.0 61.5 %shard_map.57 = (bf16[16,3,64,128]{3,2,1,0:T(8,128)(2,1)S(1)}, s32[1]{0:T(128)}) custom-call(s32[16]{0:T(128)} %occupied.1, bf16[16,32,64,128]{3,2,1,0:T(8,128)(2,1)} %bitcast.10, bf16[864,32]{1,0:T(8,128)(2,1)} %bitcast.12, bf16[864,32]{1,0:T(8,128)(2,1)} %bitcast.14, bf16[3,32]{1,0:T(4,128)(2,1)} %w_head.1), custom_call_target="tpu_custom_call" | custom-call | tf_op jit(solution)/shard_map/pallas_call | solution.py:761
  62.2 0.0 copy-done.2
  62.3 0.0 copy-done.3
  62.3 0.0 copy-done.1
  62.3 0.0 copy-done
  62.3 0.2 conditional.1
  62.5 0.9 %copy.12 = bf16[16,3,8,8,128]{4,3,2,1,0:T(8,128)(2,1)} copy(bf16[16,3,8,8,128]{4,3,2,1,0:T(8,128)(2,1)S(1)} %get-tuple-element.30) | data formatting | bytes 1572864
Async XLA Ops:
  0.0 62.2 %copy-start.2 = (bf16[3,32]{1,0:T(4,128)(2,1)S(1)}, bf16[3,32]{1,0:T(4,128)(2,1)}, u32[]{:S(2)}) copy-start(bf16[3,32]{1,0:T(4,128)(2,1)} %w_head.1) | copy-start | bytes 580
  0.0 62.3 %copy-start.3 = (s32[16]{0:T(128)S(1)}, s32[16]{0:T(128)}, u32[]{:S(2)}) copy-start(s32[16]{0:T(128)} %occupied.1) | copy-start | bytes 196
  0.0 62.3 %copy-start.1 = (bf16[32,32,3,3,3]{1,0,4,3,2:T(8,128)(2,1)S(1)}, bf16[32,32,3,3,3]{1,0,4,3,2:T(8,128)(2,1)}, u32[]{:S(2)}) copy-start(bf16[32,32,3,3,3]{1,0,4,3,2:T(8,128)(2,1)} %param.10) | copy-start | bytes 165892
  0.0 62.3 %copy-start = (bf16[32,32,3,3,3]{1,0,4,3,2:T(8,128)(2,1)S(1)}, bf16[32,32,3,3,3]{1,0,4,3,2:T(8,128)(2,1)}, u32[]{:S(2)}) copy-start(bf16[32,32,3,3,3]{1,0,4,3,2:T(8,128)(2,1)} %param.9) | copy-start | bytes 165892

commit v6 on v5

--- a/solution.py
+++ b/solution.py
@@ -352,11 +352,15 @@
 
 
 SLOTS = 7
-SURE = 3
-GROUPS = ((0, 4, 3), (4, 8, 4), (8, 10, 5))
+SURE = 2
+GROUPS = ((0, 4, 2), (4, 8, 4), (8, 10, 5))
 LANES = 10
 TWINS = 4
-TARGETS = (6, 5)
+TURNS = (
+    (6, (0, 5, 6, 1, 2, 3, 4)),
+    (5, (1, 2, 3, 4, 5, 6, 0)),
+    (5, (0, 5, 6, 1, 2, 3, 4)),
+)
 COLUMNS = 32
 
 
@@ -403,8 +407,8 @@
 def make_plan(counts, used):
     load = counts
     own = counts
-    for turn, target in enumerate(TARGETS):
-        for kind in (0, 5, 6, 1, 2, 3, 4):
+    for turn, (target, order) in enumerate(TURNS):
+        for kind in order:
             gap = load - across(load, kind, 1)
             before = used[kind].reshape(load.shape) if turn > 0 else jnp.zeros_like(load)
             if kind == 0:
@@ -417,7 +421,7 @@
             own = own - sends
             load = load - sends + across(sends, kind, -1)
     need = jnp.maximum(own, SURE)
-    for kinds, start in (((0,), 3), ((1, 2, 3, 4), 4), ((5, 6), 5)):
+    for kinds, start in (((0,), 2), ((1, 2, 3, 4), 4), ((5, 6), 5)):
         taken = jnp.zeros_like(load)
         for kind in kinds:
             taken = taken + across(used[kind].reshape(load.shape), kind, -1)
@@ -624,9 +628,13 @@
         def _():
             stage_own(s + 1)
 
+        @pl.when(s == 1)
+        def _():
+            receive(0)
+            stage(2)
+
         @pl.when(s == 2)
         def _():
-            receive(0)
             stage(3)
             send(2)
 

time: 63.5 us -> 64.1 us (level)
  Pallas kernels: 61.5 us -> 62.2 us
    pallas_call x1, Pallas kernels: 61.5 us -> 62.2 us  [on_device(): out, needed = shared(*args)]
where the time goes in v6:
time: 64.1 us; the launch traced here: 64 us
  Pallas kernels  62.2 us (97%)
  local copies, waits for them, and re-layouts  0.9 us (1%)
  between operations  0.74 us (1%)
    pallas_call x1, Pallas kernels, on_device(): out, needed = shared(*args)  62.2 us

profile of v6, /device:TPU:0, one launch (start us, length us, event | category | flops | bytes accessed | tf_op | source)
XLA Modules:
  0.0 64.0 jit_solution(12885993622994246260)
XLA Ops:
  0.0 0.0 copy-start.2
  0.0 0.0 copy-start.3
  0.0 0.0 copy-start.1
  0.0 0.0 copy-start
  0.0 62.2 %shard_map.57 = (bf16[16,3,64,128]{3,2,1,0:T(8,128)(2,1)S(1)}, s32[1]{0:T(128)}) custom-call(s32[16]{0:T(128)} %occupied.1, bf16[16,32,64,128]{3,2,1,0:T(8,128)(2,1)} %bitcast.10, bf16[864,32]{1,0:T(8,128)(2,1)} %bitcast.12, bf16[864,32]{1,0:T(8,128)(2,1)} %bitcast.14, bf16[3,32]{1,0:T(4,128)(2,1)} %w_head.1), custom_call_target="tpu_custom_call" | custom-call | tf_op jit(solution)/shard_map/pallas_call | solution.py:769
  62.9 0.0 copy-done.2
  62.9 0.0 copy-done.3
  62.9 0.0 copy-done.1
  62.9 0.0 copy-done
  62.9 0.2 conditional.1
  63.1 0.9 %copy.12 = bf16[16,3,8,8,128]{4,3,2,1,0:T(8,128)(2,1)} copy(bf16[16,3,8,8,128]{4,3,2,1,0:T(8,128)(2,1)S(1)} %get-tuple-element.30) | data formatting | bytes 1572864
Async XLA Ops:
  0.0 62.9 %copy-start.2 = (bf16[3,32]{1,0:T(4,128)(2,1)S(1)}, bf16[3,32]{1,0:T(4,128)(2,1)}, u32[]{:S(2)}) copy-start(bf16[3,32]{1,0:T(4,128)(2,1)} %w_head.1) | copy-start | bytes 580
  0.0 62.9 %copy-start.3 = (s32[16]{0:T(128)S(1)}, s32[16]{0:T(128)}, u32[]{:S(2)}) copy-start(s32[16]{0:T(128)} %occupied.1) | copy-start | bytes 196
  0.0 62.9 %copy-start.1 = (bf16[32,32,3,3,3]{1,0,4,3,2:T(8,128)(2,1)S(1)}, bf16[32,32,3,3,3]{1,0,4,3,2:T(8,128)(2,1)}, u32[]{:S(2)}) copy-start(bf16[32,32,3,3,3]{1,0,4,3,2:T(8,128)(2,1)} %param.10) | copy-start | bytes 165892
  0.0 62.9 %copy-start = (bf16[32,32,3,3,3]{1,0,4,3,2:T(8,128)(2,1)S(1)}, bf16[32,32,3,3,3]{1,0,4,3,2:T(8,128)(2,1)}, u32[]{:S(2)}) copy-start(bf16[32,32,3,3,3]{1,0,4,3,2:T(8,128)(2,1)} %param.9) | copy-start | bytes 165892
